TPU v7x, 256 devices: a whole 4x4x8 slice. The times are simulated.
256 devices in a mesh: bead: 32 (over z_hi, x, core), dom: 8 (over y, z_lo).
Axes of the slice: x: 4, y: 4, z: 8 (z_hi: 4, z_lo: 2; z = z_hi * 2 + z_lo), core: 2. Of those that a mesh axis runs over, the one named last changes fastest.
Arguments:
- positions: float32 [3, 32, 4096], P(None, 'bead', 'dom'), may hold values from -2.5 to 2.5
- momenta: float32 [3, 32, 4096], P(None, 'bead', 'dom'), may hold values from -6 to 6
- forces: float32 [3, 32, 4096], P(None, 'bead', 'dom'), may hold values from -6 to 6
- masses: float32 [4096], P('dom'), may hold values from 1 to 16
- charges: float32 [4096], P('dom'), may hold values from -1 to 1
- embedding: bfloat16 [4096, 240], P('dom'), may hold values from -6 to 6
- neighbours: int32 [8, 4096], P(None, 'dom'), may hold values from 0 to 895
- send_rows: int32 [3072], P('dom'), may hold values from 0 to 511
- wavevectors: int32 [3, 16384], replicated, may hold values from -12 to 12, as said below
- radial_weight: bfloat16 [2, 16, 240], replicated, may hold values from -1.5 to 1.5
- mix_weight: bfloat16 [2, 240, 240], replicated, may hold values from -0.375 to 0.375
- update_weight: bfloat16 [2, 240, 240], replicated, may hold values from -0.375 to 0.375
- readout_weight: bfloat16 [240, 240], replicated, may hold values from -0.375 to 0.375
- energy_weight: float32 [240], replicated, may hold values from -0.375 to 0.375
Outputs:
- next_positions: float32 [3, 32, 4096], P(None, 'bead', 'dom')
- next_momenta: float32 [3, 32, 4096], P(None, 'bead', 'dom')
- next_forces: float32 [3, 32, 4096], P(None, 'bead', 'dom')
Inputs may be any that keep to these rules, and one draw needn't show every extreme that they name: `wavevectors`: no component is zero.
All inputs are finite; a program needn't handle non-finite values.
Results may differ from a plain program's by a relative error of at most 0.0065.
Values may be sent and summed in bfloat16 or wider, within the bound.
A program may use at most 64 MiB of HBM per device.

v0:
```python
import math

import jax
import jax.numpy as jnp
from jax import lax
from jax.sharding import PartitionSpec as P

step_dt = 0.25
omega_cycle = 1.6
box_length = 4.0
ewald_sigma = 0.002
ewald_gain = 48.0
norm_eps = 1e-06
peak_frequency = lax.Precision.HIGHEST


def extended(cells, sides, width):
    for axis, dim in sides:
        count = lax.axis_size(axis)
        head = lax.slice_in_dim(cells, 0, width, axis=dim)
        tail = lax.slice_in_dim(cells, cells.shape[dim] - width, cells.shape[dim], axis=dim)
        cells = jnp.concatenate(
            [
                lax.ppermute(tail, axis, [(i, (i + 1) % count) for i in range(count)]),
                cells,
                lax.ppermute(head, axis, [((i + 1) % count, i) for i in range(count)]),
            ],
            axis=dim,
        )
    return cells


def mode_matrix(length):
    row_index = jnp.arange(length, dtype=jnp.int32)[:, None]
    column_index = jnp.arange(length, dtype=jnp.int32)[None, :]
    angles = 2.0 * math.pi / length * (row_index * column_index % length).astype(jnp.float32)
    single_norm = math.sqrt(1.0 / length)
    double_norm = math.sqrt(2.0 / length)
    parity = (1 - 2 * (row_index % 2)).astype(jnp.float32)
    middle = length // 2
    normal_transform = jnp.where(
        column_index == 0,
        single_norm,
        jnp.where(
            column_index < middle,
            double_norm * jnp.cos(angles),
            jnp.where(column_index == middle, single_norm * parity, double_norm * jnp.sin(angles)),
        ),
    )
    return normal_transform


def propagate(normal_mode_positions, normal_mode_momentum, masses):
    length = normal_mode_positions.shape[1]
    orders = jnp.arange(length, dtype=jnp.float32)
    omegas = 2.0 * omega_cycle * jnp.sin(math.pi * orders / length)
    cosine = jnp.cos(omegas * step_dt)[:, None]
    sines = jnp.sin(omegas * step_dt)
    omega_safe = jnp.where(orders == 0.0, 1.0, omegas)
    drift = jnp.where(orders == 0.0, step_dt, sines / omega_safe)[:, None]
    spring = (omegas * sines)[:, None]
    next_coords = cosine * normal_mode_positions + drift * normal_mode_momentum / masses
    next_moment = cosine * normal_mode_momentum - spring * masses * normal_mode_positions
    return (next_coords, next_moment)


def ewald_coef(reciprocal, atom_total):
    square = jnp.sum(reciprocal * reciprocal, 0)
    return (
        ewald_gain
        / math.sqrt(reciprocal.shape[1] * atom_total)
        * jnp.exp(-ewald_sigma * square)
        / square
    )


def phase_sums(reciprocal, centre, charge):
    phases = jnp.dot(reciprocal.T, centre, precision=peak_frequency)
    return (
        jnp.dot(jnp.cos(phases), charge, precision=peak_frequency),
        jnp.dot(jnp.sin(phases), charge, precision=peak_frequency),
    )


def ewald_force(reciprocal, centre, charge, cosine_sum, sine_sum, damping):
    phases = jnp.dot(reciprocal.T, centre, precision=peak_frequency)
    weight = (damping * cosine_sum)[:, None] * jnp.sin(phases) - (damping * sine_sum)[
        :, None
    ] * jnp.cos(phases)
    return 2.0 * charge * jnp.dot(reciprocal, weight, precision=peak_frequency)


def long_range(reciprocal, centre, charge, damping):
    cosine_part, sine_part = phase_sums(reciprocal, centre, charge)
    cosine_sum, sine_sum = lax.psum((cosine_part, sine_part), ("bead", "dom"))
    return ewald_force(reciprocal, centre, charge, cosine_sum, sine_sum, damping)


def advance(normal_mode_entries, mass_share, charge_share, reciprocal, damping):
    normal_mode_positions, normal_mode_momentum = propagate(
        normal_mode_entries[:3], normal_mode_entries[3:], mass_share
    )
    centre = normal_mode_positions[:, 0, :] / math.sqrt(normal_mode_entries.shape[1])
    long_force = long_range(reciprocal, centre, charge_share, damping)
    return (jnp.concatenate([normal_mode_positions, normal_mode_momentum], 0), long_force)


def layer_apply(
    hidden_own,
    extended_rows,
    extended_coords,
    neighbour_table,
    radial,
    mixing,
    update,
    radial_rates,
):
    owned_count = hidden_own.shape[0]
    owners = extended_coords[:, :owned_count]
    others = extended_coords[:, neighbour_table]
    offset = others - owners[:, None, :]
    distance = jnp.sum(offset * offset, 0)
    basis = (1.0 / (1.0 + radial_rates[:, None, None] * distance[None])).astype(jnp.bfloat16)
    edge_weight = jnp.einsum("mka,mf->kaf", basis, radial, preferred_element_type=jnp.float32)
    message = jnp.sum(edge_weight * extended_rows[neighbour_table], 0)
    scaled = message * lax.rsqrt(jnp.mean(message * message, -1, keepdims=True) + norm_eps)
    gated = jax.nn.silu(
        jnp.dot(scaled.astype(jnp.bfloat16), mixing, preferred_element_type=jnp.float32)
    ).astype(jnp.bfloat16)
    return hidden_own + jnp.dot(gated, update, preferred_element_type=jnp.float32)


def readout(hidden, readout_weight, energy_weight):
    activation = jax.nn.silu(
        jnp.dot(hidden.astype(jnp.bfloat16), readout_weight, preferred_element_type=jnp.float32)
    )
    return jnp.sum(activation * energy_weight)


def short_forces(
    coords,
    embedding,
    neighbours,
    send_rows,
    radial_weight,
    mix_weight,
    update_weight,
    readout_weight,
    energy_weight,
):
    owned_rows = coords.shape[2]
    ghost_rows = send_rows.shape[0] // 2
    to_before = send_rows[:ghost_rows]
    to_after = send_rows[ghost_rows:]
    radial_rates = 0.125 * 2.0 ** (0.5 * jnp.arange(radial_weight.shape[1], dtype=jnp.float32))
    apply_layer = jax.vmap(layer_apply, in_axes=(0, 0, 0, None, None, None, None, None))
    beside_all = extended(coords[:, :, send_rows], (("dom", 2),), ghost_rows)
    extended_coords = jnp.concatenate(
        [coords, beside_all[:, :, :ghost_rows], beside_all[:, :, 3 * ghost_rows :]], 2
    )
    extended_coords = jnp.moveaxis(extended_coords, 1, 0)
    hidden = embedding.astype(jnp.float32)[None]
    stored = []
    for number in range(mix_weight.shape[0]):
        rounded = hidden.astype(jnp.bfloat16)
        arrived = extended(rounded[:, send_rows, :], (("dom", 1),), ghost_rows)
        extended_rows = jnp.concatenate(
            [rounded, arrived[:, :ghost_rows], arrived[:, 3 * ghost_rows :]], 1
        ).astype(jnp.float32)
        stored.append((hidden, extended_rows))
        hidden = apply_layer(
            hidden,
            extended_rows,
            extended_coords,
            neighbours,
            radial_weight[number],
            mix_weight[number],
            update_weight[number],
            radial_rates,
        )
    cotan = jax.vmap(jax.grad(readout), in_axes=(0, None, None))(
        hidden, readout_weight, energy_weight
    )
    position_grad = jnp.zeros_like(extended_coords)
    for number in reversed(range(mix_weight.shape[0])):
        layer_input, extended_rows = stored[number]

        def local_layer(hidden_part, rows_part, coords_part):
            return apply_layer(
                hidden_part,
                rows_part,
                coords_part,
                neighbours,
                radial_weight[number],
                mix_weight[number],
                update_weight[number],
                radial_rates,
            )

        unused, pullback = jax.vjp(local_layer, layer_input, extended_rows, extended_coords)
        input_grad, feature_grad, position_part = pullback(cotan)
        position_grad = position_grad + position_part
        if number > 0:
            returned = extended(
                feature_grad[:, owned_rows:, :].astype(jnp.bfloat16), (("dom", 1),), ghost_rows
            ).astype(jnp.float32)
            owned_grad = (
                feature_grad[:, :owned_rows, :]
                .at[:, to_before, :]
                .add(returned[:, :ghost_rows])
                .at[:, to_after, :]
                .add(returned[:, 3 * ghost_rows :])
            )
            cotan = input_grad + owned_grad.astype(jnp.bfloat16).astype(jnp.float32)
    returned = extended(position_grad[:, :, owned_rows:], (("dom", 2),), ghost_rows)
    owned_force = (
        position_grad[:, :, :owned_rows]
        .at[:, :, to_before]
        .add(returned[:, :, :ghost_rows])
        .at[:, :, to_after]
        .add(returned[:, :, 3 * ghost_rows :])
    )
    return -jnp.moveaxis(owned_force, 0, 1)


def local(
    positions,
    momenta,
    forces,
    masses,
    charges,
    embedding,
    neighbours,
    send_rows,
    wavevectors,
    radial_weight,
    mix_weight,
    update_weight,
    readout_weight,
    energy_weight,
):
    beads_here = positions.shape[1]
    atom_count = positions.shape[2]
    bead_devices = lax.axis_size("bead")
    bead_slot = lax.axis_index("bead")
    bead_count = beads_here * bead_devices
    atom_share = atom_count // bead_devices
    normal_transform = mode_matrix(bead_count)
    bead_rows = lax.dynamic_slice_in_dim(normal_transform, bead_slot * beads_here, beads_here, 0)
    mass_share = lax.dynamic_slice_in_dim(masses, bead_slot * atom_share, atom_share, 0)
    charge_share = lax.dynamic_slice_in_dim(charges, bead_slot * atom_share, atom_share, 0)
    reciprocal = wavevectors.astype(jnp.float32) * (2.0 * math.pi / box_length)
    damping = ewald_coef(reciprocal, atom_count * lax.axis_size("dom"))
    coords_now, moment_now, force_now = (positions, momenta, forces)
    kicked = moment_now + 0.5 * step_dt * force_now
    stacked_arrays = jnp.concatenate([coords_now, kicked], 0)
    segment = stacked_arrays
    summed = lax.psum_scatter(
        jnp.einsum("bk,cba->ack", bead_rows, segment, precision=peak_frequency),
        "bead",
        scatter_dimension=0,
        tiled=True,
    )
    normal_mode_entries = jnp.transpose(summed, (1, 2, 0))
    joined, long_force = advance(normal_mode_entries, mass_share, charge_share, reciprocal, damping)
    packed = jnp.concatenate(
        [jnp.transpose(joined, (2, 0, 1)).reshape(atom_share, 6 * bead_count), long_force.T], 1
    )
    segment = lax.all_gather(packed, "bead", axis=0, tiled=True)
    row_count = segment.shape[0]
    coords = segment[:, : 6 * bead_count].reshape(row_count, 6, bead_count)
    restored = jnp.einsum("bk,ack->cba", bead_rows, coords, precision=peak_frequency)
    spread = segment[:, 6 * bead_count :].T[:, None, :]
    arrived = jnp.concatenate([restored, spread], 0)
    coords_now = arrived[:3]
    short_force = short_forces(
        coords_now,
        embedding,
        neighbours,
        send_rows,
        radial_weight,
        mix_weight,
        update_weight,
        readout_weight,
        energy_weight,
    )
    force_now = short_force + arrived[6:]
    moment_now = arrived[3:6] + 0.5 * step_dt * force_now
    return (coords_now, moment_now, force_now)


def solution(mesh):
    placed = (
        P(None, "bead", "dom"),
        P(None, "bead", "dom"),
        P(None, "bead", "dom"),
        P("dom"),
        P("dom"),
        P("dom", None),
        P(None, "dom"),
        P("dom"),
        P(),
        P(),
        P(),
        P(),
        P(),
        P(),
    )
    return jax.shard_map(
        local,
        mesh=mesh,
        in_specs=placed,
        out_specs=(P(None, "bead", "dom"), P(None, "bead", "dom"), P(None, "bead", "dom")),
        check_vma=False,
    )
```

profile of v0, /device:TPU:1, one launch (start us, length us, event | category | flops | bytes accessed | tf_op | source)
XLA Modules:
  0.0 635.9 jit_solution(1569555388232173794)
XLA Ops:
  14.6 5.0 collective-permute-start.3
  21.6 84.1 %reduce-scatter.2.cloned.1.call-done = f32[16,6,32]{2,1,0:T(8,128)} async-done(((f32[512,6,32]{2,1,0:T(8,128)}), f32[16,6,32]{2,1,0:T(8,128)}) %reduce-scatter.2.cloned.1.call-update) | async-done | bytes 12304 | tf_op jit(solution)/shard_map/reduce_scatter | solution.py:258
  106.8 8.0 %fusion.207 = (f32[16384,16]{0,1:T(8,128)S(1)}, f32[16384,16]{0,1:T(8,128)S(1)}) fusion(f32[3,16]{1,0:T(4,128)S(1)} %fusion.160, s32[3,16384]{1,0:T(4,128)S(1)} %copy-done.11), kind=kOutput, calls=%fused_computation.258 | convolution fusion | flops 9535488 | bytes 2293952 | tf_op jit(solution)/shard_map/dot_general | solution.py:78
  117.5 240.5 %all-reduce.5.cloned.1.call-done = (f32[16384]{0:T(1024)}, f32[16384]{0:T(1024)}) async-done(((f32[16384]{0:T(1024)}, f32[16384]{0:T(1024)}), (f32[16384]{0:T(1024)}, f32[16384]{0:T(1024)})) %all-reduce.5.cloned.1.call-update) | async-done | bytes 131088 | tf_op jit(solution)/shard_map/psum | solution.py:95
  360.5 43.3 %all_gather.3 = f32[512,195]{1,0:T(8,128)S(1)} all-gather(f32[16,195]{1,0:T(8,128)S(1)} %pad_maximum_fusion.5), channel_id=1, replica_groups=mesh['bead'=32,'dom'=8] {'bead'}, dimensions={0}, use_global_device_ids=true | all-gather | bytes 411840 | tf_op jit(solution)/shard_map/all_gather | solution.py:269
  405.7 2.1 collective-permute-start.1
  408.1 16.1 %gather_fusion.3 = f32[4096,240]{1,0:T(8,128)} fusion(f32[896,240]{1,0:T(8,128)S(1)} %fusion.95, s32[4096]{0:T(1024)S(1)} %broadcast_clamp_fusion), kind=kCustom, calls=%fused_computation.3 | custom fusion | bytes 7880704 | tf_op jit(solution)/shard_map/vmap()/gather | solution.py:125
  424.1 5.3 copy.144
  429.4 5.3 copy.134
  435.5 10.8 %gather_fusion.1 = f32[4096,3]{1,0:T(8,128)S(1)} fusion(f32[3,896]{0,1:T(8,128)S(1)} %get-tuple-element.32, s32[4096]{0:T(1024)S(1)} %broadcast_clamp_fusion), kind=kCustom, calls=%fused_computation.1 | custom fusion | bytes 114688 | tf_op jit(solution)/shard_map/jvp(vmap())/gather | solution.py:120
  447.0 2.9 multiply_reduce_fusion.1
  454.0 3.6 collective-permute-start.5
  457.8 2.6 fusion.124
  460.4 3.2 collective-permute-done.4
  466.1 16.1 %gather_fusion.5 = f32[4096,240]{1,0:T(8,128)} fusion(f32[896,240]{1,0:T(8,128)S(1)} %copy.137, s32[4096]{0:T(1024)S(1)} %broadcast_clamp_fusion), kind=kCustom, calls=%fused_computation.5 | custom fusion | bytes 7880704 | tf_op jit(solution)/shard_map/vmap()/gather | solution.py:125
  482.1 5.3 copy.139
  487.5 4.4 multiply_reduce_fusion
  492.9 2.6 fusion.13
  495.5 2.1 convolution_convert_fusion.4
  497.7 2.5 multiply_reduce_fusion.4
  502.1 4.7 broadcast_multiply_fusion
  506.8 5.2 copy.154
  512.0 23.1 %scatter_custom_fusion.1 = f32[896,240]{1,0:T(8,128)S(1)} fusion(s32[4096]{0:T(1024)S(1)} %bitcast.302, f32[4096,240]{1,0:T(8,128)} %bitcast.291, f32[]{:T(128)} %constant.51.clone.1), kind=kCustom, calls=%fused_computation.103 | custom fusion | flops 983040 | bytes 860672 | tf_op jit(solution)/shard_map/transpose(jvp(vmap()))/scatter-add | solution.py:125
  538.2 5.3 copy.140
  543.5 3.1 fusion.59
  548.5 3.9 scatter_custom_fusion.2
  552.4 3.5 scatter_custom_fusion.3
  557.0 2.5 multiply_reduce_fusion.3
  560.7 2.8 fusion.38
  563.6 3.1 add_multiply_fusion
  571.6 22.8 %scatter_fusion = f32[3,896]{0,1:T(8,128)S(1)} fusion(f32[3,896]{0,1:T(8,128)S(1)} %pad_bitcast_fusion.1, s32[4096]{0:T(1024)S(1)} %bitcast.303, f32[4096,3]{1,0:T(8,128)} %bitcast.288), kind=kCustom, calls=%fused_computation.6 | custom fusion | flops 12288 | bytes 163840 | tf_op jit(solution)/shard_map/transpose(jvp(vmap()))/scatter-add | solution.py:120
  594.4 21.9 %scatter_fusion.1 = f32[3,896]{0,1:T(8,128)} fusion(f32[3,896]{0,1:T(8,128)} %pad_bitcast_fusion, s32[4096]{0:T(1024)S(1)} %bitcast.304, f32[4096,3]{1,0:T(8,128)S(1)} %bitcast.287), kind=kCustom, calls=%fused_computation.10 | custom fusion | flops 12288 | bytes 163840 | tf_op jit(solution)/shard_map/transpose(jvp(vmap()))/scatter-add | solution.py:120
  (166 shorter events, 52.9 us)
Async XLA Ops:
  7.2 485.8 %copy-start = (bf16[240,240]{1,0:T(8,128)(2,1)S(1)}, bf16[240,240]{1,0:T(8,128)(2,1)}, u32[]{:S(2)}) copy-start(bf16[240,240]{1,0:T(8,128)(2,1)} %param.26) | copy-start | bytes 345604
  7.2 5.2 copy-start.14
  7.2 5.3 copy-start.26
  7.2 13.3 %copy-start.21 = (s32[8,512]{1,0:T(8,128)S(1)}, s32[8,512]{1,0:T(8,128)}, u32[]{:S(2)}) copy-start(s32[8,512]{1,0:T(8,128)} %param.20) | copy-start | bytes 49156
  7.2 13.3 %copy-start.27 = (f32[512]{0:T(512)S(1)}, f32[512]{0:T(512)}, u32[]{:S(2)}) copy-start(f32[512]{0:T(512)} %param.18) | copy-start | bytes 6148
  7.2 14.1 %copy-start.11 = (s32[3,16384]{1,0:T(4,128)S(1)}, s32[3,16384]{1,0:T(4,128)}, u32[]{:S(2)}) copy-start(s32[3,16384]{1,0:T(4,128)} %param.22) | copy-start | bytes 589828
  7.2 98.5 %reduce-scatter.2.cloned.1.call-start = ((), (), s32[]{:S(2)}) async-start(), calls=%async_computation.1 | async-start | bytes 2162688 | tf_op jit(solution)/shard_map/reduce_scatter | solution.py:258
  12.3 345.7 %all-reduce.5.cloned.1.call-start = ((), (), s32[]{:S(2)}) async-start(), calls=%async_computation.2 | async-start | bytes 262144 | tf_op jit(solution)/shard_map/psum | solution.py:95
  14.6 393.3 %collective-permute-start.3 = (bf16[1,192,240]{2,1,0:T(8,128)(2,1)S(1)}, bf16[1,192,240]{2,1,0:T(8,128)(2,1)S(1)}, u32[]{:S(2)}, u32[]{:S(2)}) collective-permute-start(bf16[1,192,240]{2,1,0:T(8,128)(2,1)S(1)} %get-tuple-element.38), channel_id=1, source_target_pairs={{1,0},{2,1},{3,2},{4,3},{5,4},{6,5},{7,6},{0,7},{9,8},{10,9},{11,1... | collective-permute-start | bytes 276488 | tf_op jit(solution)/shard_map/ppermute | solution.py:26
  19.6 388.3 %collective-permute-start.2 = (bf16[1,192,240]{2,1,0:T(8,128)(2,1)S(1)}, bf16[1,192,240]{2,1,0:T(8,128)(2,1)S(1)}, u32[]{:S(2)}, u32[]{:S(2)}) collective-permute-start(bf16[1,192,240]{2,1,0:T(8,128)(2,1)S(1)} %get-tuple-element.37), channel_id=1, source_target_pairs={{0,1},{1,2},{2,3},{3,4},{4,5},{5,6},{6,7},{7,0},{8,9},{9,10},{10,1... | collective-permute-start | bytes 276488 | tf_op jit(solution)/shard_map/ppermute | solution.py:24
  19.8 427.2 %copy-start.22 = (f32[16]{0:T(128)}, f32[16]{0:T(128)S(1)}, u32[]{:S(2)}) copy-start(f32[16]{0:T(128)S(1)} %power_multiply_fusion) | copy-start | bytes 196
  403.8 4.2 copy-start.6
  405.7 29.8 %collective-permute-start.1 = (f32[3,1,192]{0,2,1:T(8,128)S(1)}, f32[3,1,192]{0,2,1:T(8,128)S(1)}, u32[]{:S(2)}, u32[]{:S(2)}) collective-permute-start(f32[3,1,192]{0,2,1:T(8,128)S(1)} %get-tuple-element.36), channel_id=1, source_target_pairs={{1,0},{2,1},{3,2},{4,3},{5,4},{6,5},{7,6},{0,7},{9,8},{10,9},{11,1... | collective-permute-start | bytes 6920 | tf_op jit(solution)/shard_map/ppermute | solution.py:26
  407.8 27.7 %collective-permute-start = (f32[3,1,192]{0,2,1:T(8,128)S(1)}, f32[3,1,192]{0,2,1:T(8,128)S(1)}, u32[]{:S(2)}, u32[]{:S(2)}) collective-permute-start(f32[3,1,192]{0,2,1:T(8,128)S(1)} %get-tuple-element.35), channel_id=1, source_target_pairs={{0,1},{1,2},{2,3},{3,4},{4,5},{5,6},{6,7},{7,0},{8,9},{9,10},{10,1... | collective-permute-start | bytes 6920 | tf_op jit(solution)/shard_map/ppermute | solution.py:24
  434.7 12.3 %copy-start.18 = (bf16[2,16,240]{2,1,0:T(8,128)(2,1)S(1)}, bf16[2,16,240]{2,1,0:T(8,128)(2,1)}, u32[]{:S(2)}) copy-start(bf16[2,16,240]{2,1,0:T(8,128)(2,1)} %param.23) | copy-start | bytes 46084
  446.4 3.9 copy-start.15
  446.4 3.9 copy-start.28
  449.9 7.8 %copy-start.23 = (f32[16]{0:T(128)S(1)}, f32[16]{0:T(128)}, u32[]{:S(2)}) copy-start(f32[16]{0:T(128)} %copy-done.22) | copy-start | bytes 196
  450.0 10.4 %copy-start.19 = (f32[512]{0:T(512)}, f32[512]{0:T(512)S(1)}, u32[]{:S(2)}) copy-start(f32[512]{0:T(512)S(1)} %multiply_reduce_fusion.6) | copy-start | bytes 6148
  454.0 6.4 %collective-permute-start.5 = (bf16[1,192,240]{1,2,0:T(8,128)(2,1)S(1)}, bf16[1,192,240]{1,2,0:T(8,128)(2,1)S(1)}, u32[]{:S(2)}, u32[]{:S(2)}) collective-permute-start(bf16[1,192,240]{1,2,0:T(8,128)(2,1)S(1)} %get-tuple-element.40), channel_id=1, source_target_pairs={{1,0},{2,1},{3,2},{4,3},{5,4},{6,5},{7,6},{0,7},{9,8},{10,9},{11,1... | collective-permute-start | bytes 276488 | tf_op jit(solution)/shard_map/ppermute | solution.py:26
  457.6 6.0 collective-permute-start.4
  487.5 4.4 copy-start.17
  536.8 11.7 %collective-permute-start.7 = (bf16[1,192,240]{2,1,0:T(8,128)(2,1)}, bf16[1,192,240]{2,1,0:T(8,128)(2,1)S(1)}, u32[]{:S(2)}, u32[]{:S(2)}) collective-permute-start(bf16[1,192,240]{2,1,0:T(8,128)(2,1)} %get-tuple-element.30), channel_id=1, source_target_pairs={{1,0},{2,1},{3,2},{4,3},{5,4},{6,5},{7,6},{0,7},{9,8},{10,9},{11,1... | collective-permute-start | bytes 276488 | tf_op jit(solution)/shard_map/ppermute | solution.py:26
  537.1 11.3 %collective-permute-start.6 = (bf16[1,192,240]{2,1,0:T(8,128)(2,1)}, bf16[1,192,240]{2,1,0:T(8,128)(2,1)}, u32[]{:S(2)}, u32[]{:S(2)}) collective-permute-start(bf16[1,192,240]{2,1,0:T(8,128)(2,1)} %get-tuple-element.29), channel_id=1, source_target_pairs={{0,1},{1,2},{2,3},{3,4},{4,5},{5,6},{6,7},{7,0},{8,9},{9,10},{10,1... | collective-permute-start | bytes 276488 | tf_op jit(solution)/shard_map/ppermute | solution.py:24
  538.2 5.3 copy-start.24
  543.5 13.5 %copy-start.3 = (f32[512,240]{0,1:T(8,128)S(1)}, f32[512,240]{0,1:T(8,128)}, u32[]{:S(2)}) copy-start(f32[512,240]{0,1:T(8,128)} %copy-done.2) | copy-start | bytes 1474564
  546.6 12.9 %copy-start.20 = (f32[512]{0:T(512)S(1)}, f32[512]{0:T(512)}, u32[]{:S(2)}) copy-start(f32[512]{0:T(512)} %copy-done.19) | copy-start | bytes 6148
  548.5 12.3 %copy-start.25 = (f32[16]{0:T(128)S(1)}, f32[16]{0:T(128)}, u32[]{:S(2)}) copy-start(f32[16]{0:T(128)} %copy-done.22) | copy-start | bytes 196
  568.9 57.9 %copy-start.7 = (f32[512,195]{1,0:T(8,128)S(1)}, f32[512,195]{1,0:T(8,128)}, u32[]{:S(2)}) copy-start(f32[512,195]{1,0:T(8,128)} %copy-done.6) | copy-start | bytes 1198084
  568.9 57.9 %copy-start.10 = (f32[1,512,6]{2,1,0:T(8,128)S(1)}, f32[1,512,6]{2,1,0:T(8,128)}, u32[]{:S(2)}) copy-start(f32[1,512,6]{2,1,0:T(8,128)} %copy-done.9) | copy-start | bytes 36868
  617.4 5.7 collective-permute-start.8
  619.2 5.8 collective-permute-start.9
  (10 other events, 23.8 us)
Sparse Core Ops, SparseCore 0:
  12.4 93.2 reduce-scatter.1
  117.5 240.4 all-reduce.4
where the time goes:
time: 645 us; the launch traced here: 636 us
  waiting for transfers between devices  330 us (51%)
  other arithmetic  107 us (17%)
  local copies, waits for them, and re-layouts  88.1 us (14%)
  blocking collectives  43.3 us (7%)
  matrix products  35.9 us (6%)
  starting transfers between devices  16.3 us (3%)
  between operations  15.3 us (2%)
    psum x1, waiting for transfers between devices, long_range(): cosine_sum, sine_sum = lax.psum((cosine_part, sine_part), ('bead', 'dom'))  240 us
    reduce_scatter x1, waiting for transfers between devices, local(): lax.psum_scatter(jnp.einsum('bk,cba->ack', bead_rows, segment, precision=...  84.1 us
    gather x6, local copies, waits for them, and re-layouts, layer_apply(): message = jnp.sum(edge_weight * extended_rows[neighbour_table], 0)  53.4 us
    scatter-add x2, other arithmetic, layer_apply(): others = extended_coords[:, neighbour_table]  44.7 us
    all_gather x1, blocking collectives, local(): segment = lax.all_gather(packed, 'bead', axis=0, tiled=True)  43.3 us
    scatter-add x1, other arithmetic, layer_apply(): message = jnp.sum(edge_weight * extended_rows[neighbour_table], 0)  23.1 us
    ppermute x5, starting transfers between devices, extended(): lax.ppermute(head, axis, [((i + 1) % count, i) for i in range(count)])  13 us
  transfers between devices with their start and end apart: 12, of which 4 were waited for; matrix products, arithmetic and copies ran while one was open for 10% of the time, Pallas kernels for 0%

commit v1 on v0

v1 whole, which is shorter than its diff:
```python
import math

import jax
import jax.numpy as jnp
import numpy as np
from jax import lax
from jax.experimental import pallas as pl
from jax.experimental.pallas import tpu as pltpu
from jax.sharding import PartitionSpec as P

MESH = pl.DeviceIdType.MESH
F32 = jnp.float32
BF16 = jnp.bfloat16

BEADS = 32
ATOMS = 512
TOTAL_ATOMS = 4096
GHOST = 192
SIDE = 256
EXT = ATOMS + 2 * SIDE
NEIGH = 8
FEAT = 240
BASIS = 16
KVEC = 16384
KPART = KVEC // BEADS
DT = 0.25
TWO_PI = 2.0 * math.pi

S1, EMB, PACK, MA, MB, GH, FG, DG, SK, E1, E2, XP, FO, GG, N_SEMS = np.cumsum(
    [0, 8, 1, 1, 4, 4, 8, 4, 2, 8, 8, 4, 1, 1, 2]
).tolist()


def ring_tables():
    k = np.arange(BEADS)
    b = np.arange(BEADS)[:, None]
    angle = 2.0 * np.pi / BEADS * (b * k % BEADS)
    half = BEADS // 2
    basis = np.where(k < half, np.cos(angle), np.sin(angle)) * math.sqrt(2.0 / BEADS)
    basis = np.where(k == 0, math.sqrt(1.0 / BEADS), basis)
    basis = np.where(k == half, math.sqrt(1.0 / BEADS) * (1 - 2 * (b % 2)), basis)
    omega = 3.2 * np.sin(np.pi * k / BEADS)
    cosine, sine = np.cos(omega * DT), np.sin(omega * DT)
    drift = np.where(k == 0, DT, sine / np.where(k == 0, 1.0, omega))
    rows = [(basis * value) @ basis.T for value in (cosine, drift, omega * sine)]
    return np.concatenate([row[0] for row in rows]).astype(np.float32)


def dot(a, b):
    return lax.dot_general(a, b, (((1,), (0,)), ((), ())), preferred_element_type=F32)


def dot_t(a, b):
    return lax.dot_general(a, b, (((1,), (1,)), ((), ())), preferred_element_type=F32)


def rows_of(shape):
    return lax.broadcasted_iota(jnp.int32, shape, 0)


def lanes_of(shape):
    return lax.broadcasted_iota(jnp.int32, shape, 1)


def two_parts(value):
    high = value.astype(BF16)
    return high, (value - high.astype(F32)).astype(BF16)


def stacked_parts(value):
    high = value.astype(BF16).astype(F32)
    return jnp.concatenate([high, value - high], 0).astype(BF16)


def lane_pick(tables, index):
    result = None
    for number, block in enumerate(tables):
        local = index - 128 * number
        inside = jnp.logical_and(local >= 0, local < 128)
        got = jnp.take_along_axis(block, jnp.where(inside, local, 0), axis=1, mode="promise_in_bounds")
        result = jnp.where(inside, got, 0.0 if result is None else result)
    return result


def step_kernel(
    coef,
    pos,
    mom,
    force,
    mass,
    charge,
    emb,
    neigh,
    send,
    wave,
    radial,
    mix,
    update,
    readout,
    ew,
    out_pos,
    out_mom,
    out_force,
    v_own,
    v_all,
    emb_buf,
    pack_own,
    pack_buf,
    ma_send,
    ma_buf,
    mb_send,
    mb_buf,
    gh_send,
    gh_buf,
    fg_send,
    fg_buf,
    dg_send,
    dg_buf,
    sk_buf,
    e1_buf,
    e2_buf,
    xp_send,
    xp_buf,
    fo_send,
    fo_buf,
    gg_send,
    gg_buf,
    sel,
    sel_own,
    onehot,
    ext_rows,
    picked,
    d_picked,
    basis_buf,
    slope_buf,
    dist_buf,
    ddist_buf,
    offset_buf,
    msg,
    dmsg,
    drows,
    hidden,
    pre_buf,
    normed_buf,
    inv_buf,
    mix_t,
    update_t,
    readout_t,
    radial_t,
    wave_buf,
    wave_t,
    r_buf,
    cos_buf,
    sin_buf,
    send_sem,
    recv_sem,
):
    bead = lax.axis_index("bead")
    dom = lax.axis_index("dom")
    z, x, core = bead // 8, (bead // 2) % 4, bead % 2
    y, low = dom // 2, dom % 2
    ring = 2 * y + core

    def dev(z_, x_, y_, low_, core_):
        return ((z_ * 4 + x_) * 2 + core_, y_ * 2 + low_)

    def ring_dev(z_, step):
        place = (ring + step) % 8
        return dev(z_, x, place // 2, low, place % 2)

    def swapped_ring_dev(step):
        place = (ring + step) % 8
        return dev(z, x, place // 2, place % 2, low)

    def copy(src, dst, send_at, recv_at, target):
        return pltpu.make_async_remote_copy(
            src_ref=src,
            dst_ref=dst,
            send_sem=send_sem.at[send_at],
            recv_sem=recv_sem.at[recv_at],
            device_id=target,
            device_id_type=MESH,
        )

    def arrive(dst, recv_at):
        copy(dst, dst, 0, recv_at, dev(z, x, y, low, 1 - core)).wait_recv()

    started = []

    def send_to(src, dst, send_at, recv_at, target):
        out = copy(src, dst, send_at, recv_at, target)
        out.start()
        started.append(out)

    same = low == core
    conditional = []

    def send_or_keep(src, dst, send_at, recv_at, target):
        out = copy(src, dst, send_at, recv_at, target)

        @pl.when(same)
        def _():
            pltpu.make_async_copy(src, dst, recv_sem.at[recv_at]).start()

        @pl.when(jnp.logical_not(same))
        def _():
            out.start()

        conditional.append(out)

    barrier = pltpu.get_barrier_semaphore()
    greeted = []
    for dx in range(4):
        for dl in range(2):
            for dc in range(2):
                if dx or dl or dc:
                    greeted.append(dev(z, (x + dx) % 4, y, (low + dl) % 2, (core + dc) % 2))
    for dy in range(1, 4):
        for dc in range(2):
            greeted.append(dev(z, x, (y + dy) % 4, low, (core + dc) % 2))
    for dz in range(1, 4):
        for step in (-1, 0, 1):
            greeted.append(ring_dev((z + dz) % 4, step + 8))
    greeted.append(dev(z, x, (y + jnp.where(core == 0, 3, 1)) % 4, 1 - core, low))
    greeted.append(dev(z, x, (y + jnp.where(low == 0, 3, 1)) % 4, core, 1 - low))
    for target in greeted:
        pl.semaphore_signal(barrier, inc=1, device_id=target, device_id_type=MESH)

    v_own[...] = jnp.zeros((8, ATOMS), F32)
    for c in range(3):
        v_own[c : c + 1, :] = pos[c]
        v_own[4 + c : 5 + c, :] = mom[c] + (0.5 * DT) * force[c]
    lane = lanes_of((1, 2 * SIDE))
    rows384 = jnp.concatenate([send[...], jnp.zeros((1, 128), jnp.int32)], 1)
    shifted = pltpu.roll(rows384, 64, 1)
    spread = jnp.where(
        lane < GHOST,
        rows384,
        jnp.where(jnp.logical_and(lane >= SIDE, lane < SIDE + GHOST), shifted, -1),
    ).astype(F32)
    table = neigh[...]
    pack_own[0:8, :] = jnp.where(table >= ATOMS + GHOST, table + (SIDE - GHOST), table).astype(F32)
    pack_own[8:9, :] = mass[...]
    pack_own[9:10, :] = charge[...]
    pack_own[10:11, :] = spread
    pack_own[11:16, :] = jnp.zeros((5, ATOMS), F32)
    pl.semaphore_wait(barrier, len(greeted))

    slot = x * 2 + core
    send_or_keep(v_own, v_all.at[slot], S1, S1 + slot, dev(z, x, y, low, low))
    for number in range(1, 8):
        dx, dl = number // 2, number % 2
        send_to(
            v_own,
            v_all.at[slot],
            S1 + number,
            S1 + slot,
            dev(z, (x + dx) % 4, y, (low + dl) % 2, low),
        )
    swap = dev(z, x, y, core, low)
    send_or_keep(pack_own, pack_buf, PACK, PACK, swap)
    send_or_keep(emb, emb_buf, EMB, EMB, swap)

    eye = (rows_of((FEAT, FEAT)) == lanes_of((FEAT, FEAT))).astype(F32)
    eye_b = eye.astype(BF16)
    for layer in range(2):
        mix_t[layer] = dot_t(eye_b, mix[layer]).astype(BF16)
        update_t[layer] = dot_t(eye_b, update[layer]).astype(BF16)
        radial_t[layer] = dot_t(eye_b, radial[layer]).astype(BF16)
    readout_t[...] = dot_t(eye_b, readout[...]).astype(BF16)
    ew_col = jnp.sum(eye * ew[...], axis=1, keepdims=True)
    own_spread = jnp.broadcast_to(spread, (ATOMS, 2 * SIDE))
    atom_rows = rows_of((ATOMS, 2 * SIDE)).astype(F32)
    sel_own[...] = jnp.where(own_spread == atom_rows, 1.0, 0.0).astype(BF16)
    k_first = pl.multiple_of((bead - core + low) * KPART, KPART)
    triple = wave[:, pl.ds(k_first, KPART)].astype(F32)
    wave_buf[...] = jnp.zeros((16, KPART), F32)
    for part in range(3):
        wave_buf[4 * part : 4 * part + 3, :] = triple
    wave_t[...] = jnp.transpose(wave_buf[...]).astype(BF16)

    arrive(pack_buf, PACK)
    inv_mass = 1.0 / pack_buf[8:9, :]
    charges = pack_buf[9:10, :]
    send_row = pack_buf[10:11, :]
    sel[...] = jnp.where(jnp.broadcast_to(send_row, (ATOMS, 2 * SIDE)) == atom_rows, 1.0, 0.0).astype(BF16)
    send_index = jnp.broadcast_to(send_row, (8, 2 * SIDE)).astype(jnp.int32)

    for k in range(8):
        arrive(v_all.at[k], S1 + k)
    row8 = rows_of((8, ATOMS))
    upper = row8 < 4
    scale = jnp.where(upper, inv_mass, -pack_buf[8:9, :])
    beads_in = [v_all[k] for k in range(8)]
    total = beads_in[0]
    for k in range(1, 8):
        total = total + beads_in[k]
    centre_part = (total + DT * inv_mass * pltpu.roll(total, 4, 0)) * (1.0 / BEADS)
    centre_low = pltpu.roll(centre_part, 4, 0)
    first_row = rows_of((8, 1)) < 4
    for dz in (1, 2, 3, 0):
        z_to = (z + dz) % 4
        straight = None
        for k in range(8):
            shift = (8 * (z_to - z) + 2 * x + low - k + 64) % BEADS
            same_kind = coef[shift] * beads_in[k]
            other = jnp.where(first_row, coef[2 * BEADS + shift], coef[BEADS + shift]) * beads_in[k]
            straight = same_kind if straight is None else straight + same_kind
            crossed = other if k == 0 else crossed + other
        moved = straight + scale * pltpu.roll(crossed, 4, 0)
        ma = jnp.where(upper, moved, centre_low)
        for c in range(3):
            blocks = [
                jnp.broadcast_to(moved[c : c + 1, 128 * n : 128 * n + 128], (8, 128)) for n in range(4)
            ]
            for n in range(4):
                got = lane_pick(blocks, send_index[:, 128 * n : 128 * n + 128])
                gh_send[dz, n // 2, c : c + 1, 128 * (n % 2) : 128 * (n % 2) + 128] = got[0:1]
        gh_send[dz, :, 3:4, :] = jnp.zeros((2, 1, SIDE), F32)
        if dz:
            ma_send[dz] = ma
            mb_send[dz] = moved[4:8]
            send_to(ma_send.at[dz], ma_buf.at[z], MA + dz, MA + z, ring_dev(z_to, 0))
        else:
            ma_buf[z] = ma
            mb_buf[z] = moved[4:8]
        send_to(gh_send.at[dz, 0], gh_buf.at[1, z], GH + 2 * dz, GH + 4 + z, ring_dev(z_to, 7))
        send_to(gh_send.at[dz, 1], gh_buf.at[0, z], GH + 2 * dz + 1, GH + z, ring_dev(z_to, 1))
    for dz in range(1, 4):
        send_to(mb_send.at[dz], mb_buf.at[z], MB + dz, MB + z, ring_dev((z + dz) % 4, 0))

    def send_features(layer, rounded):
        ghosts = dot(rounded, sel[...]).astype(BF16)
        fg_send[layer, 0] = ghosts[:, :SIDE]
        fg_send[layer, 1] = ghosts[:, SIDE:]
        send_to(
            fg_send.at[layer, 0], fg_buf.at[layer, 1], FG + 2 * layer, FG + 2 * layer + 1, ring_dev(z, 7)
        )
        send_to(
            fg_send.at[layer, 1], fg_buf.at[layer, 0], FG + 2 * layer + 1, FG + 2 * layer, ring_dev(z, 1)
        )

    def receive_features(layer):
        for side in range(2):
            arrive(fg_buf.at[layer, side], FG + 2 * layer + side)
            ext_rows[:, ATOMS + SIDE * side : ATOMS + SIDE * (side + 1)] = fg_buf[layer, side]

    arrive(emb_buf, EMB)
    rounded = emb_buf[...]
    hidden[...] = rounded.astype(F32)
    ext_rows[:, :ATOMS] = rounded
    send_features(0, rounded)

    group_rows = [(rows_of((16, ATOMS)) + 16 * g).astype(F32) for g in range(8)]

    def build(j, carry):
        index = pack_buf[pl.ds(j, 1), :]
        at = pl.multiple_of(j * ATOMS, ATOMS)
        for block in range(EXT // 128):
            local = jnp.broadcast_to(index - 128.0 * block, (16, ATOMS))
            for g in range(8):
                first = 128 * block + 16 * g
                onehot[first : first + 16, pl.ds(at, ATOMS)] = jnp.where(
                    local == group_rows[g], 1.0, 0.0
                ).astype(BF16)
        return carry

    lax.fori_loop(0, NEIGH, build, 0)

    def gather(layer):
        def body(j, carry):
            at = pl.multiple_of(j * ATOMS, ATOMS)
            picked[layer, j] = dot(ext_rows[...], onehot[:, pl.ds(at, ATOMS)]).astype(BF16)
            return carry

        lax.fori_loop(0, NEIGH, body, 0)

    receive_features(0)
    gather(0)

    for dz in range(1, 4):
        arrive(ma_buf.at[(z + dz) % 4], MA + (z + dz) % 4)
    for k in range(4):
        for side in range(2):
            arrive(gh_buf.at[side, k], GH + 4 * side + k)
    moved = (ma_buf[0] + ma_buf[1]) + (ma_buf[2] + ma_buf[3])
    centre = moved[4:7]
    xp_send[...] = moved
    ghosts_at = [(gh_buf[n, 0] + gh_buf[n, 1]) + (gh_buf[n, 2] + gh_buf[n, 3]) for n in range(2)]
    index8 = pack_buf[0:8, :].astype(jnp.int32)
    distance = None
    for c in range(3):
        blocks = [moved[c : c + 1, 128 * n : 128 * n + 128] for n in range(4)]
        for side in range(2):
            blocks += [ghosts_at[side][c : c + 1, 128 * n : 128 * n + 128] for n in range(2)]
        blocks = [jnp.broadcast_to(block, (8, 128)) for block in blocks]
        others = jnp.concatenate(
            [lane_pick(blocks, index8[:, 128 * n : 128 * n + 128]) for n in range(4)], 1
        )
        offset = others - moved[c : c + 1, :]
        offset_buf[c] = offset
        distance = offset * offset if c == 0 else distance + offset * offset
    dist_buf[...] = distance
    m_row = rows_of((BASIS, ATOMS))
    rates = jnp.where(m_row % 2 == 1, 0.125 * math.sqrt(2.0), 0.125) * jnp.left_shift(1, m_row // 2).astype(F32)
    for j in range(NEIGH):
        exact = 1.0 / (1.0 + rates * dist_buf[j : j + 1, :])
        basis_buf[j] = exact.astype(BF16)
        slope_buf[j] = -rates * exact * exact

    turns = centre * 0.25
    high = turns.astype(BF16).astype(F32)
    rest = turns - high
    middle = rest.astype(BF16).astype(F32)
    r_buf[...] = jnp.zeros((16, ATOMS), F32)
    for number, value in enumerate((high, middle, rest - middle)):
        r_buf[4 * number : 4 * number + 3, :] = value

    def ewald_sums():
        phase = r_buf[...].astype(BF16)

        def body(i, carry):
            at = pl.multiple_of(i * 128, 128)
            turn = dot(wave_t[pl.ds(at, 128), :], phase)
            half = (turn - jnp.round(turn)) * math.pi
            q = half * half
            s = half * (
                1.0
                + q
                * (
                    -1.6666666641e-1
                    + q * (8.3333293858e-3 + q * (-1.9840083133e-4 + q * (2.7523971075e-6 - 2.3868346521e-8 * q)))
                )
            )
            c = 1.0 + q * (
                -0.5
                + q
                * (
                    4.1666666658e-2
                    + q
                    * (
                        -1.3888888388e-3
                        + q * (2.4801544910e-5 + q * (-2.7556993055e-7 + 2.0737354e-9 * q))
                    )
                )
            )
            sin_buf[pl.ds(at, 128), :] = (2.0 * s * c).astype(BF16)
            cos_buf[pl.ds(at, 128), :] = (1.0 - 2.0 * s * s).astype(BF16)
            return carry

        lax.fori_loop(0, KPART // 128, body, 0)
        weights = stacked_parts(jnp.broadcast_to(charges, (8, ATOMS)))
        for number, ref in enumerate((cos_buf, sin_buf)):
            sums = dot_t(weights, ref[...])
            sk_buf[ring, number : number + 1, :] = sums[0:1] + sums[8:9]
        for step in range(1, 8):
            send_to(sk_buf.at[ring], sk_buf.at[ring], SK + step, SK + ring, ring_dev(z, step))

    def ewald_forces():
        for step in range(1, 8):
            place = (ring + step) % 8
            arrive(sk_buf.at[place], SK + place)
        sums = sk_buf[0]
        for k in range(1, 8):
            sums = sums + sk_buf[k]
        recip = wave_buf[0:8, :] * (TWO_PI / 4.0)
        recip = jnp.where(row8 < 3, recip, 0.0)
        square = jnp.sum(recip * recip, axis=0, keepdims=True)
        damping = 48.0 / math.sqrt(KVEC * TOTAL_ATOMS) * jnp.exp(-0.002 * square) / square
        from_sin = stacked_parts(recip * (damping * sums[0:1]))
        from_cos = stacked_parts(recip * (damping * sums[1:2]))
        part = dot(from_sin, sin_buf[...]) - dot(from_cos, cos_buf[...])
        part = 2.0 * charges * (part[0:8] + part[8:16])
        place = 2 * x + low
        e1_buf[place] = part[0:4]
        for number in range(1, 8):
            dx, dl = number // 2, number % 2
            send_to(
                e1_buf.at[place],
                e1_buf.at[place],
                E1 + number,
                E1 + place,
                dev(z, (x + dx) % 4, y, (low + dl) % 2, core),
            )

    def ewald_group_sum():
        for number in range(1, 8):
            place = 2 * ((x + number // 2) % 4) + (low + number % 2) % 2
            arrive(e1_buf.at[place], E1 + place)
        part = e1_buf[0]
        for k in range(1, 8):
            part = part + e1_buf[k]
        e2_buf[z] = part
        for dz in range(1, 4):
            send_to(e2_buf.at[z], e2_buf.at[z], E2 + dz, E2 + z, ring_dev((z + dz) % 4, 0))

    def ewald_total():
        for dz in range(1, 4):
            arrive(e2_buf.at[(z + dz) % 4], E2 + (z + dz) % 4)
        return (e2_buf[0] + e2_buf[1]) + (e2_buf[2] + e2_buf[3])

    def finish_layer(layer):
        msg[...] = jnp.zeros((FEAT, ATOMS), F32)

        def body(j, carry):
            edge = dot(radial_t[layer], basis_buf[j])
            msg[...] += edge * picked[layer, j].astype(F32)
            return carry

        lax.fori_loop(0, NEIGH, body, 0)
        message = msg[...]
        inverse = lax.rsqrt(jnp.sum(message * message, axis=0, keepdims=True) * (1.0 / FEAT) + 1e-6)
        normed = message * inverse
        normed_buf[layer] = normed
        inv_buf[layer] = jnp.broadcast_to(inverse, (8, ATOMS))
        pre = dot(mix_t[layer], normed.astype(BF16))
        pre_buf[layer] = pre
        gated = (pre * lax.logistic(pre)).astype(BF16)
        hidden[...] += dot(update_t[layer], gated)

    finish_layer(0)
    rounded = hidden[...].astype(BF16)
    ext_rows[:, :ATOMS] = rounded
    send_features(1, rounded)
    ewald_sums()
    for dz in range(1, 4):
        arrive(mb_buf.at[(z + dz) % 4], MB + (z + dz) % 4)
    xp_send[4:8, :] = (mb_buf[0] + mb_buf[1]) + (mb_buf[2] + mb_buf[3])
    send_or_keep(xp_send, xp_buf, XP, XP, swap)
    receive_features(1)
    gather(1)
    finish_layer(1)

    def silu_slope(pre):
        sig = lax.logistic(pre)
        return sig * (1.0 + pre * (1.0 - sig))

    final = dot(readout_t[...], hidden[...].astype(BF16))
    dfinal = ew_col * silu_slope(final)
    cotan = dot(readout[...], dfinal.astype(BF16)).astype(BF16)

    def message_cotan(layer, cotan_b):
        dgated = dot(update[layer], cotan_b).astype(BF16).astype(F32)
        dpre = dgated * silu_slope(pre_buf[layer])
        dnormed = dot(mix[layer], dpre.astype(BF16)).astype(BF16).astype(F32)
        normed = normed_buf[layer]
        mean = jnp.sum(dnormed * normed, axis=0, keepdims=True) * (1.0 / FEAT)
        dmsg[...] = inv_buf[layer, 0:1, :] * (dnormed - normed * mean)

    def distance_cotan(layer):
        def body(j, carry):
            dedge = (picked[layer, j].astype(F32) * dmsg[...]).astype(BF16)
            dbasis = dot(radial[layer], dedge).astype(BF16).astype(F32)
            part = jnp.sum(dbasis * slope_buf[j], axis=0, keepdims=True)
            if layer == 1:
                ddist_buf[pl.ds(j, 1), :] = part
            else:
                ddist_buf[pl.ds(j, 1), :] += part
            return carry

        lax.fori_loop(0, NEIGH, body, 0)

    message_cotan(1, cotan)

    def row_cotan(j, carry):
        at = pl.multiple_of(j * ATOMS, ATOMS)
        edge = dot(radial_t[1], basis_buf[j])
        d_picked[:, pl.ds(at, ATOMS)] = (edge * dmsg[...]).astype(BF16)
        return carry

    lax.fori_loop(0, NEIGH, row_cotan, 0)
    for side in range(2):
        first = ATOMS + SIDE * side
        dg_send[side] = dot_t(d_picked[...], onehot[first : first + SIDE, :]).astype(BF16)
        send_to(dg_send.at[side], dg_buf.at[1 - side], DG + side, DG + 1 - side, ring_dev(z, 7 if side == 0 else 1))
    for half in range(2):
        drows[:, SIDE * half : SIDE * half + SIDE] = dot_t(
            d_picked[...], onehot[SIDE * half : SIDE * half + SIDE, :]
        )
    distance_cotan(1)
    ewald_forces()
    for side in range(2):
        arrive(dg_buf.at[side], DG + side)
    returned = dot_t(dg_buf[0], sel[:, :SIDE]) + dot_t(dg_buf[1], sel[:, SIDE:])
    owned = (drows[...] + returned).astype(BF16).astype(F32)
    ewald_group_sum()
    message_cotan(0, (cotan.astype(F32) + owned).astype(BF16))
    distance_cotan(0)

    ddist = 2.0 * ddist_buf[...]
    edge_force = [offset_buf[c] * ddist for c in range(3)]
    for c in range(3):
        own = jnp.sum(edge_force[c], axis=0, keepdims=True)
        fo_send[c : c + 1, :] = own
    fo_send[3:4, :] = jnp.zeros((1, ATOMS), F32)

    parts = []
    zero_row = jnp.zeros((1, ATOMS), F32)
    for j in range(NEIGH):
        rows = [edge_force[c][j : j + 1, :] for c in range(3)] + [zero_row] * 5
        parts.append(stacked_parts(jnp.concatenate(rows, 0)))
    force_rows = jnp.concatenate(parts, 1)
    for side in range(2):
        first = ATOMS + SIDE * side
        both = dot_t(force_rows, onehot[first : first + SIDE, :])
        gg_send[side] = both[0:4] + both[8:12]
        send_to(
            gg_send.at[side], gg_buf.at[1 - side], GG + side, GG + 1 - side, swapped_ring_dev(7 if side == 0 else 1)
        )
    both = dot_t(force_rows, onehot[:ATOMS, :])
    fo_send[...] = (fo_send[...] - (both[0:4] + both[8:12])) + ewald_total()
    send_or_keep(fo_send, fo_buf, FO, FO, swap)

    arrive(xp_buf, XP)
    for side in range(2):
        arrive(gg_buf.at[side], GG + side)
    zero4 = jnp.zeros((4, SIDE), F32)
    returned = None
    for side in range(2):
        rows = stacked_parts(jnp.concatenate([gg_buf[side], zero4], 0))
        both = dot_t(rows, sel_own[:, SIDE * side : SIDE * side + SIDE])
        both = both[0:4] + both[8:12]
        returned = both if side == 0 else returned + both
    arrive(fo_buf, FO)
    result = fo_buf[...] - returned
    for c in range(3):
        out_pos[c] = xp_buf[c : c + 1, :]
        out_mom[c] = xp_buf[4 + c : 5 + c, :] + (0.5 * DT) * result[c : c + 1, :]
        out_force[c] = result[c : c + 1, :]

    for out in started:
        out.wait_send()

    @pl.when(jnp.logical_not(same))
    def _():
        for out in conditional:
            out.wait_send()


def local(
    positions,
    momenta,
    forces,
    masses,
    charges,
    embedding,
    neighbours,
    send_rows,
    wavevectors,
    radial_weight,
    mix_weight,
    update_weight,
    readout_weight,
    energy_weight,
):
    vmem = pl.BlockSpec(memory_space=pltpu.VMEM)
    piece = jax.ShapeDtypeStruct((3, 1, ATOMS), F32)
    scratch = [
        ((8, ATOMS), F32),
        ((8, 8, ATOMS), F32),
        ((FEAT, ATOMS), BF16),
        ((16, ATOMS), F32),
        ((16, ATOMS), F32),
        ((4, 8, ATOMS), F32),
        ((4, 8, ATOMS), F32),
        ((4, 4, ATOMS), F32),
        ((4, 4, ATOMS), F32),
        ((4, 2, 4, SIDE), F32),
        ((2, 4, 4, SIDE), F32),
        ((2, 2, FEAT, SIDE), BF16),
        ((2, 2, FEAT, SIDE), BF16),
        ((2, FEAT, SIDE), BF16),
        ((2, FEAT, SIDE), BF16),
        ((8, 2, KPART), F32),
        ((8, 4, ATOMS), F32),
        ((4, 4, ATOMS), F32),
        ((8, ATOMS), F32),
        ((8, ATOMS), F32),
        ((4, ATOMS), F32),
        ((4, ATOMS), F32),
        ((2, 4, SIDE), F32),
        ((2, 4, SIDE), F32),
        ((ATOMS, 2 * SIDE), BF16),
        ((ATOMS, 2 * SIDE), BF16),
        ((EXT, NEIGH * ATOMS), BF16),
        ((FEAT, EXT), BF16),
        ((2, NEIGH, FEAT, ATOMS), BF16),
        ((FEAT, NEIGH * ATOMS), BF16),
        ((NEIGH, BASIS, ATOMS), BF16),
        ((NEIGH, BASIS, ATOMS), F32),
        ((NEIGH, ATOMS), F32),
        ((NEIGH, ATOMS), F32),
        ((3, NEIGH, ATOMS), F32),
        ((FEAT, ATOMS), F32),
        ((FEAT, ATOMS), F32),
        ((FEAT, ATOMS), F32),
        ((FEAT, ATOMS), F32),
        ((2, FEAT, ATOMS), F32),
        ((2, FEAT, ATOMS), F32),
        ((2, 8, ATOMS), F32),
        ((2, FEAT, FEAT), BF16),
        ((2, FEAT, FEAT), BF16),
        ((FEAT, FEAT), BF16),
        ((2, FEAT, BASIS), BF16),
        ((16, KPART), F32),
        ((KPART, 16), BF16),
        ((16, ATOMS), F32),
        ((KPART, ATOMS), BF16),
        ((KPART, ATOMS), BF16),
    ]
    return pl.pallas_call(
        step_kernel,
        out_shape=(piece, piece, piece),
        in_specs=[pl.BlockSpec(memory_space=pltpu.SMEM)] + [vmem] * 14,
        out_specs=(vmem, vmem, vmem),
        scratch_shapes=[pltpu.VMEM(shape, kind) for shape, kind in scratch]
        + [pltpu.SemaphoreType.DMA((N_SEMS,)), pltpu.SemaphoreType.DMA((N_SEMS,))],
        compiler_params=pltpu.CompilerParams(
            collective_id=0, has_side_effects=True, vmem_limit_bytes=48 * 1024 * 1024
        ),
        cost_estimate=pl.CostEstimate(flops=16_000_000_000, bytes_accessed=2_000_000, transcendentals=1_000_000),
    )(
        jnp.asarray(ring_tables()),
        positions,
        momenta,
        forces,
        masses.reshape(1, ATOMS),
        charges.reshape(1, ATOMS),
        embedding.T,
        neighbours,
        send_rows.reshape(1, 2 * GHOST),
        wavevectors,
        radial_weight,
        mix_weight,
        update_weight,
        readout_weight,
        energy_weight.reshape(1, FEAT),
    )


def solution(mesh):
    own = P(None, "bead", "dom")
    placed = (
        own,
        own,
        own,
        P("dom"),
        P("dom"),
        P("dom", None),
        P(None, "dom"),
        P("dom"),
        P(),
        P(),
        P(),
        P(),
        P(),
        P(),
    )
    return jax.shard_map(local, mesh=mesh, in_specs=placed, out_specs=(own, own, own), check_vma=False)
```

time: 645 us -> 71.8 us (0.11); the launches traced: 636 us -> 71.4 us
  waiting for transfers between devices: 330 us -> 0 us
  other arithmetic: 107 us -> 0 us
  local copies, waits for them, and re-layouts: 88.1 us -> 10.7 us
  Pallas kernels: 0 us -> 60 us
  blocking collectives: 43.3 us -> 0 us
  matrix products: 35.9 us -> 0 us
  starting transfers between devices: 16.3 us -> 0 us
  between operations: 15.3 us -> 0.7 us
    psum x1 -> x0, waiting for transfers between devices: 240 us -> none  [long_range(): cosine_sum, sine_sum = lax.psum((cosine_part, sine_part), ('bead', 'dom'))]
    reduce_scatter x1 -> x0, waiting for transfers between devices: 84.1 us -> none  [local(): lax.psum_scatter(jnp.einsum('bk,cba->ack', bead_rows, segment, precision=...]
    scatter-add x7 -> x0, other arithmetic: 78.9 us -> none  [the longest x2 44.7 us: layer_apply(): others = extended_coords[:, neighbour_table]]
    gather x11 -> x0, local copies, waits for them, and re-layouts: 69.5 us -> none  [the longest x6 53.4 us: layer_apply(): message = jnp.sum(edge_weight * extended_rows[neighbour_table], 0)]
    pallas_call x0 -> x1, Pallas kernels: none -> 60 us  [local(): pl.pallas_call(step_kernel, out_shape=(piece, piece, piece), in_specs=[pl...]
    all_gather x1 -> x0, blocking collectives: 43.3 us -> none  [local(): segment = lax.all_gather(packed, 'bead', axis=0, tiled=True)]
    dot_general x16 -> x0, matrix products: 35.9 us -> none  [the longest x4 11.4 us: layer_apply(): jnp.einsum('mka,mf->kaf', basis, radial, preferred_element_type=jnp.float32)]
    ppermute x10 -> x0, starting transfers between devices: 16.2 us -> none  [the longest x5 13 us: extended(): lax.ppermute(head, axis, [((i + 1) % count, i) for i in range(count)])]
  transfers between devices with their start and end apart: 12 -> 0, of which waited for: 4 -> 0; matrix products, arithmetic and copies ran while one was open for 10% -> 0% of each run, Pallas kernels for 0% -> 0%
where the time goes in v1:
time: 71.8 us; the launch traced here: 71.4 us
  Pallas kernels  60 us (84%)
  local copies, waits for them, and re-layouts  10.7 us (15%)
    pallas_call x1, Pallas kernels, local(): pl.pallas_call(step_kernel, out_shape=(piece, piece, piece), in_specs=[pl...  60 us
    unnamed x31, local copies, waits for them, and re-layouts  9.95 us

profile of v1, /device:TPU:1, one launch (start us, length us, event | category | flops | bytes accessed | tf_op | source)
XLA Modules:
  0.0 71.4 jit_solution(11361737137152814074)
XLA Ops:
  0.6 0.0 copy-start.7
  0.6 0.0 copy-start.11
  0.7 0.0 copy-start.10
  0.7 0.0 copy-start.12
  0.7 0.7 reshape.20.send
  1.4 0.0 copy-done.7
  1.4 0.0 copy-done.11
  1.4 0.0 copy-done.10
  1.4 0.0 copy-done.12
  1.4 0.0 copy-start
  1.4 0.9 %copy-done = s32[3,16384]{1,0:T(4,128)S(1)} copy-done((s32[3,16384]{1,0:T(4,128)S(1)}, s32[3,16384]{1,0:T(4,128)}, u32[]{:S(2)}) %copy-start) | copy-done | bytes 196632
  2.4 0.0 copy-start.1
  2.4 0.9 %copy-done.1 = bf16[512,240]{0,1:T(8,128)(2,1)S(1)} copy-done((bf16[512,240]{0,1:T(8,128)(2,1)S(1)}, bf16[512,240]{0,1:T(8,128)(2,1)}, u32[]{:S(2)}) %copy-start.1) | copy-done | bytes 245784
  3.3 0.0 copy-start.2
  3.3 0.9 %copy-done.2 = bf16[2,240,240]{2,1,0:T(8,128)(2,1)S(1)} copy-done((bf16[2,240,240]{2,1,0:T(8,128)(2,1)S(1)}, bf16[2,240,240]{2,1,0:T(8,128)(2,1)}, u32[]{:S(2)}) %copy-start.2) | copy-done | bytes 230424
  4.2 0.0 copy-start.3
  4.2 0.9 %copy-done.3 = bf16[2,240,240]{2,1,0:T(8,128)(2,1)S(1)} copy-done((bf16[2,240,240]{2,1,0:T(8,128)(2,1)S(1)}, bf16[2,240,240]{2,1,0:T(8,128)(2,1)}, u32[]{:S(2)}) %copy-start.3) | copy-done | bytes 230424
  5.2 0.0 copy-start.4
  5.2 0.9 %copy-done.4 = bf16[240,240]{1,0:T(8,128)(2,1)S(1)} copy-done((bf16[240,240]{1,0:T(8,128)(2,1)S(1)}, bf16[240,240]{1,0:T(8,128)(2,1)}, u32[]{:S(2)}) %copy-start.4) | copy-done | bytes 115224
  6.1 0.0 copy-start.5
  6.1 0.7 %copy-done.5 = s32[8,512]{1,0:T(8,128)S(1)} copy-done((s32[8,512]{1,0:T(8,128)S(1)}, s32[8,512]{1,0:T(8,128)}, u32[]{:S(2)}) %copy-start.5) | copy-done | bytes 16408
  6.8 0.0 copy-start.6
  6.8 0.7 %copy-done.6 = bf16[2,16,240]{2,1,0:T(8,128)(2,1)S(1)} copy-done((bf16[2,16,240]{2,1,0:T(8,128)(2,1)S(1)}, bf16[2,16,240]{2,1,0:T(8,128)(2,1)}, u32[]{:S(2)}) %copy-start.6) | copy-done | bytes 15384
  7.5 0.0 copy-start.8
  7.5 0.7 copy-done.8
  8.2 0.0 copy-start.9
  8.2 0.7 copy-done.9
  8.9 0.7 copy-done.13
  9.6 60.0 %shard_map.166 = (f32[3,1,512]{2,1,0:T(1,128)S(1)}, f32[3,1,512]{2,1,0:T(1,128)S(1)}, f32[3,1,512]{2,1,0:T(1,128)S(1)}) custom-call(f32[96]{0:T(128)S(1)} %copy-done.13, f32[3,1,512]{2,1,0:T(1,128)S(1)} %copy-done.7, f32[3,1,512]{2,1,0:T(1,128)S(1)} %copy-done.8, f32[3,1,512]{2,1,0:T(1,128)S(1)} %copy-done.9, f32[1,512]{1,0:T(1,128)S(1)} %bitcast.5, ...), custom_call_target="tpu_custom_call" | custom-call | flops 16000000000 | bytes 2000000 | tf_op jit(solution)/shard_map/pallas_call | solution.py:711
  69.6 0.6 copy.21
  70.2 0.6 copy.22
  70.8 0.6 copy.23
  (1 shorter events, 0.0 us)
Async XLA Ops:
  0.6 0.7 %copy-start.7 = (f32[3,1,512]{2,1,0:T(1,128)S(1)}, f32[3,1,512]{2,1,0:T(1,128)}, u32[]{:S(2)}) copy-start(f32[3,1,512]{2,1,0:T(1,128)} %pos.1) | copy-start | bytes 18436
  0.6 0.7 %copy-start.11 = (f32[512]{0:T(512)S(1)}, f32[512]{0:T(512)}, u32[]{:S(2)}) copy-start(f32[512]{0:T(512)} %param.19) | copy-start | bytes 6148
  0.7 0.7 %copy-start.10 = (f32[512]{0:T(512)S(1)}, f32[512]{0:T(512)}, u32[]{:S(2)}) copy-start(f32[512]{0:T(512)} %param.18) | copy-start | bytes 6148
  0.7 0.7 %copy-start.12 = (f32[240]{0:T(256)S(1)}, f32[240]{0:T(256)}, u32[]{:S(2)}) copy-start(f32[240]{0:T(256)} %param.28) | copy-start | bytes 2884
  1.4 1.0 %copy-start = (s32[3,16384]{1,0:T(4,128)S(1)}, s32[3,16384]{1,0:T(4,128)}, u32[]{:S(2)}) copy-start(s32[3,16384]{1,0:T(4,128)} %wave.1) | copy-start | bytes 589828
  2.4 0.9 %copy-start.1 = (bf16[512,240]{0,1:T(8,128)(2,1)S(1)}, bf16[512,240]{0,1:T(8,128)(2,1)}, u32[]{:S(2)}) copy-start(bf16[512,240]{0,1:T(8,128)(2,1)} %param.20) | copy-start | bytes 737284
  3.3 0.9 %copy-start.2 = (bf16[2,240,240]{2,1,0:T(8,128)(2,1)S(1)}, bf16[2,240,240]{2,1,0:T(8,128)(2,1)}, u32[]{:S(2)}) copy-start(bf16[2,240,240]{2,1,0:T(8,128)(2,1)} %mix.1) | copy-start | bytes 691204
  4.2 0.9 %copy-start.3 = (bf16[2,240,240]{2,1,0:T(8,128)(2,1)S(1)}, bf16[2,240,240]{2,1,0:T(8,128)(2,1)}, u32[]{:S(2)}) copy-start(bf16[2,240,240]{2,1,0:T(8,128)(2,1)} %update.1) | copy-start | bytes 691204
  5.2 0.9 %copy-start.4 = (bf16[240,240]{1,0:T(8,128)(2,1)S(1)}, bf16[240,240]{1,0:T(8,128)(2,1)}, u32[]{:S(2)}) copy-start(bf16[240,240]{1,0:T(8,128)(2,1)} %readout.1) | copy-start | bytes 345604
  6.1 0.7 %copy-start.5 = (s32[8,512]{1,0:T(8,128)S(1)}, s32[8,512]{1,0:T(8,128)}, u32[]{:S(2)}) copy-start(s32[8,512]{1,0:T(8,128)} %neigh.1) | copy-start | bytes 49156
  6.8 0.7 %copy-start.6 = (bf16[2,16,240]{2,1,0:T(8,128)(2,1)S(1)}, bf16[2,16,240]{2,1,0:T(8,128)(2,1)}, u32[]{:S(2)}) copy-start(bf16[2,16,240]{2,1,0:T(8,128)(2,1)} %radial.1) | copy-start | bytes 46084
  7.5 0.7 copy-start.8
  8.2 0.7 copy-start.9
  8.9 0.7 copy-start.13

commit v2 on v1

--- a/solution.py
+++ b/solution.py
@@ -26,8 +26,8 @@
 DT = 0.25
 TWO_PI = 2.0 * math.pi
 
-S1, EMB, PACK, MA, MB, GH, FG, DG, SK, E1, E2, XP, FO, GG, N_SEMS = np.cumsum(
-    [0, 8, 1, 1, 4, 4, 8, 4, 2, 8, 8, 4, 1, 1, 2]
+S1, EMB, PACK, MA, MB, GH, FG, DG, SA, SB, E1, E2, XP, FO, GG, N_SEMS = np.cumsum(
+    [0, 8, 1, 1, 4, 4, 2, 4, 2, 1, 4, 8, 4, 1, 1, 2]
 ).tolist()
 
 
@@ -83,13 +83,28 @@
 
 
 def step_kernel(
+    coef_in,
+    pos_in,
+    mom_in,
+    force_in,
+    mass_in,
+    charge_in,
+    emb,
+    neigh_in,
+    send_in,
+    wave_in,
+    radial_in,
+    mix_in,
+    update_in,
+    readout_in,
+    ew_in,
+    out,
     coef,
     pos,
     mom,
     force,
     mass,
     charge,
-    emb,
     neigh,
     send,
     wave,
@@ -98,9 +113,6 @@
     update,
     readout,
     ew,
-    out_pos,
-    out_mom,
-    out_force,
     v_own,
     v_all,
     emb_buf,
@@ -116,7 +128,8 @@
     fg_buf,
     dg_send,
     dg_buf,
-    sk_buf,
+    sa_buf,
+    sb_buf,
     e1_buf,
     e2_buf,
     xp_send,
@@ -154,6 +167,7 @@
     sin_buf,
     send_sem,
     recv_sem,
+    load_sem,
 ):
     bead = lax.axis_index("bead")
     dom = lax.axis_index("dom")
@@ -188,15 +202,38 @@
     started = []
 
     def send_to(src, dst, send_at, recv_at, target):
-        out = copy(src, dst, send_at, recv_at, target)
-        out.start()
-        started.append(out)
+        sent = copy(src, dst, send_at, recv_at, target)
+        sent.start()
+        started.append(sent)
+
+    k_first = pl.multiple_of((bead - core + low) * KPART, KPART)
+    loads = {}
+    for number, (src, dst) in enumerate(
+        (
+            (pos_in, pos),
+            (mom_in, mom),
+            (force_in, force),
+            (mass_in, mass),
+            (charge_in, charge),
+            (neigh_in, neigh),
+            (send_in, send),
+            (coef_in, coef),
+            (radial_in, radial),
+            (mix_in, mix),
+            (update_in, update),
+            (readout_in, readout),
+            (ew_in, ew),
+            (wave_in.at[:, pl.ds(k_first, KPART)], wave),
+        )
+    ):
+        loads[number] = pltpu.make_async_copy(src, dst, load_sem.at[number])
+        loads[number].start()
 
     same = low == core
     conditional = []
 
     def send_or_keep(src, dst, send_at, recv_at, target):
-        out = copy(src, dst, send_at, recv_at, target)
+        sent = copy(src, dst, send_at, recv_at, target)
 
         @pl.when(same)
         def _():
@@ -204,34 +241,38 @@
 
         @pl.when(jnp.logical_not(same))
         def _():
-            out.start()
-
-        conditional.append(out)
+            sent.start()
+
+        conditional.append(sent)
 
     barrier = pltpu.get_barrier_semaphore()
-    greeted = []
-    for dx in range(4):
-        for dl in range(2):
-            for dc in range(2):
-                if dx or dl or dc:
-                    greeted.append(dev(z, (x + dx) % 4, y, (low + dl) % 2, (core + dc) % 2))
-    for dy in range(1, 4):
-        for dc in range(2):
-            greeted.append(dev(z, x, (y + dy) % 4, low, (core + dc) % 2))
+
+    def greet(target):
+        pl.semaphore_signal(barrier, inc=1, device_id=target, device_id_type=MESH)
+
+    far = dev((z + 3 + 2 * low) % 4, x, y, 1 - low, low)
+    for number in range(1, 8):
+        greet(dev(z, (x + number // 2) % 4, y, core, (low + number % 2) % 2))
     for dz in range(1, 4):
-        for step in (-1, 0, 1):
-            greeted.append(ring_dev((z + dz) % 4, step + 8))
-    greeted.append(dev(z, x, (y + jnp.where(core == 0, 3, 1)) % 4, 1 - core, low))
-    greeted.append(dev(z, x, (y + jnp.where(low == 0, 3, 1)) % 4, core, 1 - low))
-    for target in greeted:
-        pl.semaphore_signal(barrier, inc=1, device_id=target, device_id_type=MESH)
-
+        greet(dev((z + dz) % 4, x, y, low, core))
+    for step in (1, 7, 4):
+        greet(ring_dev(z, step))
+
+    @pl.when(jnp.logical_not(same))
+    def _():
+        greet(dev(z, x, y, core, low))
+        greet(far)
+
+    for number in range(7):
+        loads[number].wait()
     v_own[...] = jnp.zeros((8, ATOMS), F32)
     for c in range(3):
         v_own[c : c + 1, :] = pos[c]
         v_own[4 + c : 5 + c, :] = mom[c] + (0.5 * DT) * force[c]
     lane = lanes_of((1, 2 * SIDE))
-    rows384 = jnp.concatenate([send[...], jnp.zeros((1, 128), jnp.int32)], 1)
+    rows384 = jnp.concatenate(
+        [send[0:1, :], send[1:2, :], send[2:3, :], jnp.zeros((1, 128), jnp.int32)], 1
+    )
     shifted = pltpu.roll(rows384, 64, 1)
     spread = jnp.where(
         lane < GHOST,
@@ -244,7 +285,7 @@
     pack_own[9:10, :] = charge[...]
     pack_own[10:11, :] = spread
     pack_own[11:16, :] = jnp.zeros((5, ATOMS), F32)
-    pl.semaphore_wait(barrier, len(greeted))
+    pl.semaphore_wait(barrier, 13 + 2 * jnp.where(same, 0, 1))
 
     slot = x * 2 + core
     send_or_keep(v_own, v_all.at[slot], S1, S1 + slot, dev(z, x, y, low, low))
@@ -258,8 +299,11 @@
             dev(z, (x + dx) % 4, y, (low + dl) % 2, low),
         )
     swap = dev(z, x, y, core, low)
-    send_or_keep(pack_own, pack_buf, PACK, PACK, swap)
-    send_or_keep(emb, emb_buf, EMB, EMB, swap)
+    send_or_keep(pack_own, pack_buf, PACK, PACK, far)
+    send_or_keep(emb, emb_buf, EMB, EMB, far)
+
+    for number in range(7, 14):
+        loads[number].wait()
 
     eye = (rows_of((FEAT, FEAT)) == lanes_of((FEAT, FEAT))).astype(F32)
     eye_b = eye.astype(BF16)
@@ -272,8 +316,7 @@
     own_spread = jnp.broadcast_to(spread, (ATOMS, 2 * SIDE))
     atom_rows = rows_of((ATOMS, 2 * SIDE)).astype(F32)
     sel_own[...] = jnp.where(own_spread == atom_rows, 1.0, 0.0).astype(BF16)
-    k_first = pl.multiple_of((bead - core + low) * KPART, KPART)
-    triple = wave[:, pl.ds(k_first, KPART)].astype(F32)
+    triple = wave[...].astype(F32)
     wave_buf[...] = jnp.zeros((16, KPART), F32)
     for part in range(3):
         wave_buf[4 * part : 4 * part + 3, :] = triple
@@ -309,14 +352,6 @@
             crossed = other if k == 0 else crossed + other
         moved = straight + scale * pltpu.roll(crossed, 4, 0)
         ma = jnp.where(upper, moved, centre_low)
-        for c in range(3):
-            blocks = [
-                jnp.broadcast_to(moved[c : c + 1, 128 * n : 128 * n + 128], (8, 128)) for n in range(4)
-            ]
-            for n in range(4):
-                got = lane_pick(blocks, send_index[:, 128 * n : 128 * n + 128])
-                gh_send[dz, n // 2, c : c + 1, 128 * (n % 2) : 128 * (n % 2) + 128] = got[0:1]
-        gh_send[dz, :, 3:4, :] = jnp.zeros((2, 1, SIDE), F32)
         if dz:
             ma_send[dz] = ma
             mb_send[dz] = moved[4:8]
@@ -324,10 +359,6 @@
         else:
             ma_buf[z] = ma
             mb_buf[z] = moved[4:8]
-        send_to(gh_send.at[dz, 0], gh_buf.at[1, z], GH + 2 * dz, GH + 4 + z, ring_dev(z_to, 7))
-        send_to(gh_send.at[dz, 1], gh_buf.at[0, z], GH + 2 * dz + 1, GH + z, ring_dev(z_to, 1))
-    for dz in range(1, 4):
-        send_to(mb_send.at[dz], mb_buf.at[z], MB + dz, MB + z, ring_dev((z + dz) % 4, 0))
 
     def send_features(layer, rounded):
         ghosts = dot(rounded, sel[...]).astype(BF16)
@@ -350,6 +381,8 @@
     hidden[...] = rounded.astype(F32)
     ext_rows[:, :ATOMS] = rounded
     send_features(0, rounded)
+    for dz in range(1, 4):
+        send_to(mb_send.at[dz], mb_buf.at[z], MB + dz, MB + z, ring_dev((z + dz) % 4, 0))
 
     group_rows = [(rows_of((16, ATOMS)) + 16 * g).astype(F32) for g in range(8)]
 
@@ -367,47 +400,35 @@
 
     lax.fori_loop(0, NEIGH, build, 0)
 
-    def gather(layer):
+    def gather_part(layer, first, last, fresh):
         def body(j, carry):
             at = pl.multiple_of(j * ATOMS, ATOMS)
-            picked[layer, j] = dot(ext_rows[...], onehot[:, pl.ds(at, ATOMS)]).astype(BF16)
+            part = dot(ext_rows[:, first:last], onehot[first:last, pl.ds(at, ATOMS)])
+            if not fresh:
+                part = part + picked[layer, j].astype(F32)
+            picked[layer, j] = part.astype(BF16)
             return carry
 
-        lax.fori_loop(0, NEIGH, body, 0)
+        lax.fori_loop(0, NEIGH, body, 0, unroll=True)
 
     receive_features(0)
-    gather(0)
+    gather_part(0, 0, EXT, True)
 
     for dz in range(1, 4):
         arrive(ma_buf.at[(z + dz) % 4], MA + (z + dz) % 4)
-    for k in range(4):
-        for side in range(2):
-            arrive(gh_buf.at[side, k], GH + 4 * side + k)
     moved = (ma_buf[0] + ma_buf[1]) + (ma_buf[2] + ma_buf[3])
     centre = moved[4:7]
     xp_send[...] = moved
-    ghosts_at = [(gh_buf[n, 0] + gh_buf[n, 1]) + (gh_buf[n, 2] + gh_buf[n, 3]) for n in range(2)]
-    index8 = pack_buf[0:8, :].astype(jnp.int32)
-    distance = None
     for c in range(3):
-        blocks = [moved[c : c + 1, 128 * n : 128 * n + 128] for n in range(4)]
-        for side in range(2):
-            blocks += [ghosts_at[side][c : c + 1, 128 * n : 128 * n + 128] for n in range(2)]
-        blocks = [jnp.broadcast_to(block, (8, 128)) for block in blocks]
-        others = jnp.concatenate(
-            [lane_pick(blocks, index8[:, 128 * n : 128 * n + 128]) for n in range(4)], 1
-        )
-        offset = others - moved[c : c + 1, :]
-        offset_buf[c] = offset
-        distance = offset * offset if c == 0 else distance + offset * offset
-    dist_buf[...] = distance
-    m_row = rows_of((BASIS, ATOMS))
-    rates = jnp.where(m_row % 2 == 1, 0.125 * math.sqrt(2.0), 0.125) * jnp.left_shift(1, m_row // 2).astype(F32)
-    for j in range(NEIGH):
-        exact = 1.0 / (1.0 + rates * dist_buf[j : j + 1, :])
-        basis_buf[j] = exact.astype(BF16)
-        slope_buf[j] = -rates * exact * exact
-
+        blocks = [
+            jnp.broadcast_to(moved[c : c + 1, 128 * n : 128 * n + 128], (8, 128)) for n in range(4)
+        ]
+        for n in range(4):
+            got = lane_pick(blocks, send_index[:, 128 * n : 128 * n + 128])
+            gh_send[n // 2, c : c + 1, 128 * (n % 2) : 128 * (n % 2) + 128] = got[0:1]
+    gh_send[:, 3:4, :] = jnp.zeros((2, 1, SIDE), F32)
+    send_to(gh_send.at[0], gh_buf.at[1], GH, GH + 1, ring_dev(z, 7))
+    send_to(gh_send.at[1], gh_buf.at[0], GH + 1, GH, ring_dev(z, 1))
     turns = centre * 0.25
     high = turns.astype(BF16).astype(F32)
     rest = turns - high
@@ -452,17 +473,45 @@
         weights = stacked_parts(jnp.broadcast_to(charges, (8, ATOMS)))
         for number, ref in enumerate((cos_buf, sin_buf)):
             sums = dot_t(weights, ref[...])
-            sk_buf[ring, number : number + 1, :] = sums[0:1] + sums[8:9]
-        for step in range(1, 8):
-            send_to(sk_buf.at[ring], sk_buf.at[ring], SK + step, SK + ring, ring_dev(z, step))
+            sa_buf[core, number : number + 1, :] = sums[0:1] + sums[8:9]
+        send_to(sa_buf.at[core], sa_buf.at[core], SA, SA, dev(z, x, y, low, 1 - core))
+
+    def ewald_ring():
+        arrive(sa_buf.at[1 - core], SA)
+        sb_buf[y] = sa_buf[0] + sa_buf[1]
+        for dy in range(1, 4):
+            send_to(sb_buf.at[y], sb_buf.at[y], SB + dy, SB + y, dev(z, x, (y + dy) % 4, low, core))
+
+    ewald_sums()
+    ghosts_at = []
+    for side in range(2):
+        arrive(gh_buf.at[side], GH + side)
+        ghosts_at.append(gh_buf[side])
+    index8 = pack_buf[0:8, :].astype(jnp.int32)
+    distance = None
+    for c in range(3):
+        blocks = [moved[c : c + 1, 128 * n : 128 * n + 128] for n in range(4)]
+        for side in range(2):
+            blocks += [ghosts_at[side][c : c + 1, 128 * n : 128 * n + 128] for n in range(2)]
+        blocks = [jnp.broadcast_to(block, (8, 128)) for block in blocks]
+        others = jnp.concatenate(
+            [lane_pick(blocks, index8[:, 128 * n : 128 * n + 128]) for n in range(4)], 1
+        )
+        offset = others - moved[c : c + 1, :]
+        offset_buf[c] = offset
+        distance = offset * offset if c == 0 else distance + offset * offset
+    dist_buf[...] = distance
+    m_row = rows_of((BASIS, ATOMS))
+    rates = jnp.where(m_row % 2 == 1, 0.125 * math.sqrt(2.0), 0.125) * jnp.left_shift(1, m_row // 2).astype(F32)
+    for j in range(NEIGH):
+        exact = 1.0 / (1.0 + rates * dist_buf[j : j + 1, :])
+        basis_buf[j] = exact.astype(BF16)
+        slope_buf[j] = -rates * exact * exact
 
     def ewald_forces():
-        for step in range(1, 8):
-            place = (ring + step) % 8
-            arrive(sk_buf.at[place], SK + place)
-        sums = sk_buf[0]
-        for k in range(1, 8):
-            sums = sums + sk_buf[k]
+        for dy in range(1, 4):
+            arrive(sb_buf.at[(y + dy) % 4], SB + (y + dy) % 4)
+        sums = (sb_buf[0] + sb_buf[1]) + (sb_buf[2] + sb_buf[3])
         recip = wave_buf[0:8, :] * (TWO_PI / 4.0)
         recip = jnp.where(row8 < 3, recip, 0.0)
         square = jnp.sum(recip * recip, axis=0, keepdims=True)
@@ -507,7 +556,7 @@
             msg[...] += edge * picked[layer, j].astype(F32)
             return carry
 
-        lax.fori_loop(0, NEIGH, body, 0)
+        lax.fori_loop(0, NEIGH, body, 0, unroll=True)
         message = msg[...]
         inverse = lax.rsqrt(jnp.sum(message * message, axis=0, keepdims=True) * (1.0 / FEAT) + 1e-6)
         normed = message * inverse
@@ -518,17 +567,19 @@
         gated = (pre * lax.logistic(pre)).astype(BF16)
         hidden[...] += dot(update_t[layer], gated)
 
+    ewald_ring()
     finish_layer(0)
     rounded = hidden[...].astype(BF16)
     ext_rows[:, :ATOMS] = rounded
     send_features(1, rounded)
-    ewald_sums()
+    gather_part(1, 0, ATOMS, True)
     for dz in range(1, 4):
         arrive(mb_buf.at[(z + dz) % 4], MB + (z + dz) % 4)
     xp_send[4:8, :] = (mb_buf[0] + mb_buf[1]) + (mb_buf[2] + mb_buf[3])
     send_or_keep(xp_send, xp_buf, XP, XP, swap)
+    ewald_forces()
     receive_features(1)
-    gather(1)
+    gather_part(1, ATOMS, EXT, False)
     finish_layer(1)
 
     def silu_slope(pre):
@@ -558,7 +609,7 @@
                 ddist_buf[pl.ds(j, 1), :] += part
             return carry
 
-        lax.fori_loop(0, NEIGH, body, 0)
+        lax.fori_loop(0, NEIGH, body, 0, unroll=True)
 
     message_cotan(1, cotan)
 
@@ -568,7 +619,7 @@
         d_picked[:, pl.ds(at, ATOMS)] = (edge * dmsg[...]).astype(BF16)
         return carry
 
-    lax.fori_loop(0, NEIGH, row_cotan, 0)
+    lax.fori_loop(0, NEIGH, row_cotan, 0, unroll=True)
     for side in range(2):
         first = ATOMS + SIDE * side
         dg_send[side] = dot_t(d_picked[...], onehot[first : first + SIDE, :]).astype(BF16)
@@ -578,12 +629,11 @@
             d_picked[...], onehot[SIDE * half : SIDE * half + SIDE, :]
         )
     distance_cotan(1)
-    ewald_forces()
+    ewald_group_sum()
     for side in range(2):
         arrive(dg_buf.at[side], DG + side)
     returned = dot_t(dg_buf[0], sel[:, :SIDE]) + dot_t(dg_buf[1], sel[:, SIDE:])
     owned = (drows[...] + returned).astype(BF16).astype(F32)
-    ewald_group_sum()
     message_cotan(0, (cotan.astype(F32) + owned).astype(BF16))
     distance_cotan(0)
 
@@ -624,17 +674,17 @@
     arrive(fo_buf, FO)
     result = fo_buf[...] - returned
     for c in range(3):
-        out_pos[c] = xp_buf[c : c + 1, :]
-        out_mom[c] = xp_buf[4 + c : 5 + c, :] + (0.5 * DT) * result[c : c + 1, :]
-        out_force[c] = result[c : c + 1, :]
-
-    for out in started:
-        out.wait_send()
+        out[c] = xp_buf[c : c + 1, :]
+        out[3 + c] = xp_buf[4 + c : 5 + c, :] + (0.5 * DT) * result[c : c + 1, :]
+        out[6 + c] = result[c : c + 1, :]
+
+    for sent in started:
+        sent.wait_send()
 
     @pl.when(jnp.logical_not(same))
     def _():
-        for out in conditional:
-            out.wait_send()
+        for sent in conditional:
+            sent.wait_send()
 
 
 def local(
@@ -653,9 +703,21 @@
     readout_weight,
     energy_weight,
 ):
-    vmem = pl.BlockSpec(memory_space=pltpu.VMEM)
-    piece = jax.ShapeDtypeStruct((3, 1, ATOMS), F32)
+    piece = (3, 1, ATOMS)
     scratch = [
+        (piece, F32),
+        (piece, F32),
+        (piece, F32),
+        ((1, ATOMS), F32),
+        ((1, ATOMS), F32),
+        ((NEIGH, ATOMS), jnp.int32),
+        ((3, 128), jnp.int32),
+        ((3, KPART), jnp.int32),
+        ((2, BASIS, FEAT), BF16),
+        ((2, FEAT, FEAT), BF16),
+        ((2, FEAT, FEAT), BF16),
+        ((FEAT, FEAT), BF16),
+        ((1, FEAT), F32),
         ((8, ATOMS), F32),
         ((8, 8, ATOMS), F32),
         ((FEAT, ATOMS), BF16),
@@ -665,13 +727,14 @@
         ((4, 8, ATOMS), F32),
         ((4, 4, ATOMS), F32),
         ((4, 4, ATOMS), F32),
-        ((4, 2, 4, SIDE), F32),
-        ((2, 4, 4, SIDE), F32),
+        ((2, 4, SIDE), F32),
+        ((2, 4, SIDE), F32),
         ((2, 2, FEAT, SIDE), BF16),
         ((2, 2, FEAT, SIDE), BF16),
         ((2, FEAT, SIDE), BF16),
         ((2, FEAT, SIDE), BF16),
-        ((8, 2, KPART), F32),
+        ((2, 2, KPART), F32),
+        ((4, 2, KPART), F32),
         ((8, 4, ATOMS), F32),
         ((4, 4, ATOMS), F32),
         ((8, ATOMS), F32),
@@ -708,15 +771,20 @@
         ((KPART, ATOMS), BF16),
         ((KPART, ATOMS), BF16),
     ]
-    return pl.pallas_call(
+    out = pl.pallas_call(
         step_kernel,
-        out_shape=(piece, piece, piece),
-        in_specs=[pl.BlockSpec(memory_space=pltpu.SMEM)] + [vmem] * 14,
-        out_specs=(vmem, vmem, vmem),
-        scratch_shapes=[pltpu.VMEM(shape, kind) for shape, kind in scratch]
-        + [pltpu.SemaphoreType.DMA((N_SEMS,)), pltpu.SemaphoreType.DMA((N_SEMS,))],
+        out_shape=jax.ShapeDtypeStruct((9, 1, ATOMS), F32),
+        in_specs=[pl.BlockSpec(memory_space=pltpu.HBM)] * 15,
+        out_specs=pl.BlockSpec(memory_space=pltpu.VMEM),
+        scratch_shapes=[pltpu.SMEM((3 * BEADS,), F32)]
+        + [pltpu.VMEM(shape, kind) for shape, kind in scratch]
+        + [
+            pltpu.SemaphoreType.DMA((N_SEMS,)),
+            pltpu.SemaphoreType.DMA((N_SEMS,)),
+            pltpu.SemaphoreType.DMA((14,)),
+        ],
         compiler_params=pltpu.CompilerParams(
-            collective_id=0, has_side_effects=True, vmem_limit_bytes=48 * 1024 * 1024
+            collective_id=0, has_side_effects=True, vmem_limit_bytes=60 * 1024 * 1024
         ),
         cost_estimate=pl.CostEstimate(flops=16_000_000_000, bytes_accessed=2_000_000, transcendentals=1_000_000),
     )(
@@ -728,7 +796,7 @@
         charges.reshape(1, ATOMS),
         embedding.T,
         neighbours,
-        send_rows.reshape(1, 2 * GHOST),
+        send_rows.reshape(3, 128),
         wavevectors,
         radial_weight,
         mix_weight,
@@ -736,6 +804,7 @@
         readout_weight,
         energy_weight.reshape(1, FEAT),
     )
+    return out[0:3], out[3:6], out[6:9]
 
 
 def solution(mesh):

time: 71.8 us -> 50.9 us (0.71)
  Pallas kernels: 60 us -> 48.7 us
  local copies, waits for them, and re-layouts: 10.7 us -> 1.33 us
    pallas_call x1, Pallas kernels: 60 us -> 48.7 us  [local(): pl.pallas_call(step_kernel, out_shape=jax.ShapeDtypeStruct((9, 1, ATOMS),...]
    unnamed x31 -> x0, local copies, waits for them, and re-layouts: 9.95 us -> none
    slice x0 -> x1, local copies, waits for them, and re-layouts: none -> 1.33 us  [local(): return (out[0:3], out[3:6], out[6:9])]
where the time goes in v2:
time: 50.9 us; the launch traced here: 50.7 us
  Pallas kernels  48.7 us (96%)
  local copies, waits for them, and re-layouts  1.33 us (3%)
  between operations  0.65 us (1%)
    pallas_call x1, Pallas kernels, local(): pl.pallas_call(step_kernel, out_shape=jax.ShapeDtypeStruct((9, 1, ATOMS),...  48.7 us
    slice x1, local copies, waits for them, and re-layouts, local(): return (out[0:3], out[3:6], out[6:9])  1.33 us

profile of v2, /device:TPU:1, one launch (start us, length us, event | category | flops | bytes accessed | tf_op | source)
XLA Modules:
  0.0 50.7 jit_solution(10335376813665857714)
XLA Ops:
  0.6 48.7 %shard_map.166 = f32[9,1,512]{2,1,0:T(1,128)} custom-call(f32[96]{0:T(128)} %constant.2.clone.coef_in, f32[3,1,512]{2,1,0:T(1,128)} %pos_in.1, f32[3,1,512]{2,1,0:T(1,128)} %mom_in.1, f32[3,1,512]{2,1,0:T(1,128)} %force_in.1, f32[1,512]{1,0:T(1,128)} %bitcast.6, f32[1,512]{1,0:T(1,128)} %bitcast.7, bf16[240,512]{1,0:T(8,128)(2,1)} %bitcast.5, ...), custom_call_target="tpu_custom_call" | custom-call | flops 16000000000 | bytes 2000000 | tf_op jit(solution)/shard_map/pallas_call | solution.py:774
  49.4 1.3 %fusion = (f32[3,1,512]{2,1,0:T(1,128)}, f32[3,1,512]{2,1,0:T(1,128)}, f32[3,1,512]{2,1,0:T(1,128)}) fusion(f32[9,1,512]{2,1,0:T(1,128)} %shard_map.166), kind=kLoop, calls=%fused_computation | loop fusion | bytes 36864 | tf_op jit(solution)/shard_map/slice | solution.py:807

commit v3 on v2

--- a/solution.py
+++ b/solution.py
@@ -25,6 +25,7 @@
 KPART = KVEC // BEADS
 DT = 0.25
 TWO_PI = 2.0 * math.pi
+PACKED = FEAT + 128
 
 S1, EMB, PACK, MA, MB, GH, FG, DG, SA, SB, E1, E2, XP, FO, GG, N_SEMS = np.cumsum(
     [0, 8, 1, 1, 4, 4, 2, 4, 2, 1, 4, 8, 4, 1, 1, 2]
@@ -128,6 +129,7 @@
     fg_buf,
     dg_send,
     dg_buf,
+    dg_rows,
     sa_buf,
     sb_buf,
     e1_buf,
@@ -251,17 +253,20 @@
         pl.semaphore_signal(barrier, inc=1, device_id=target, device_id_type=MESH)
 
     far = dev((z + 3 + 2 * low) % 4, x, y, 1 - low, low)
-    for number in range(1, 8):
-        greet(dev(z, (x + number // 2) % 4, y, core, (low + number % 2) % 2))
-    for dz in range(1, 4):
+    for dz in (2, 1, 3):
         greet(dev((z + dz) % 4, x, y, low, core))
-    for step in (1, 7, 4):
-        greet(ring_dev(z, step))
+    greet(ring_dev(z, 4))
+    for dx, flip in ((2, 1), (2, 0), (1, 1), (3, 1), (1, 0), (3, 0)):
+        greet(dev(z, (x + dx) % 4, y, core, (low + flip) % 2))
 
     @pl.when(jnp.logical_not(same))
     def _():
+        greet(far)
         greet(dev(z, x, y, core, low))
-        greet(far)
+
+    greet(ring_dev(z, 7 - 6 * core))
+    greet(dev(z, x, y, core, 1 - low))
+    greet(ring_dev(z, 1 + 6 * core))
 
     for number in range(7):
         loads[number].wait()
@@ -288,16 +293,15 @@
     pl.semaphore_wait(barrier, 13 + 2 * jnp.where(same, 0, 1))
 
     slot = x * 2 + core
-    send_or_keep(v_own, v_all.at[slot], S1, S1 + slot, dev(z, x, y, low, low))
-    for number in range(1, 8):
-        dx, dl = number // 2, number % 2
+    for dx, dl in ((2, 1), (2, 0), (1, 1), (3, 1), (1, 0), (3, 0), (0, 1)):
         send_to(
             v_own,
             v_all.at[slot],
-            S1 + number,
+            S1 + 2 * dx + dl,
             S1 + slot,
             dev(z, (x + dx) % 4, y, (low + dl) % 2, low),
         )
+    send_or_keep(v_own, v_all.at[slot], S1, S1 + slot, dev(z, x, y, low, low))
     swap = dev(z, x, y, core, low)
     send_or_keep(pack_own, pack_buf, PACK, PACK, far)
     send_or_keep(emb, emb_buf, EMB, EMB, far)
@@ -341,7 +345,7 @@
     centre_part = (total + DT * inv_mass * pltpu.roll(total, 4, 0)) * (1.0 / BEADS)
     centre_low = pltpu.roll(centre_part, 4, 0)
     first_row = rows_of((8, 1)) < 4
-    for dz in (1, 2, 3, 0):
+    for dz in (2, 1, 3, 0):
         z_to = (z + dz) % 4
         straight = None
         for k in range(8):
@@ -360,21 +364,34 @@
             ma_buf[z] = ma
             mb_buf[z] = moved[4:8]
 
+    def pack_side(ref, value):
+        ref[0:FEAT, :] = value[:, 0:128].astype(BF16)
+        rest = jnp.concatenate([value[128:FEAT, 128:SIDE], jnp.zeros((256 - FEAT, 128), F32)], 0)
+        ref[FEAT:PACKED, :] = (value[0:128, 128:SIDE] + pltpu.roll(rest, 64, 1)).astype(BF16)
+
+    def unpack_side(ref, packed, first):
+        ref[:, first : first + 128] = packed[0:FEAT, :]
+        rest = packed[FEAT:PACKED, :].astype(F32)
+        ref[0:128, first + 128 : first + SIDE] = rest.astype(BF16)
+        ref[128:FEAT, first + 128 : first + SIDE] = pltpu.roll(rest, 64, 1)[0 : FEAT - 128].astype(BF16)
+
+    def send_sides(src, dst, first_sem):
+        for near in range(2):
+            side = core if near == 0 else 1 - core
+            send_to(
+                src.at[side], dst.at[1 - side], first_sem + side, first_sem + 1 - side, ring_dev(z, 7 - 6 * side)
+            )
+
     def send_features(layer, rounded):
-        ghosts = dot(rounded, sel[...]).astype(BF16)
-        fg_send[layer, 0] = ghosts[:, :SIDE]
-        fg_send[layer, 1] = ghosts[:, SIDE:]
-        send_to(
-            fg_send.at[layer, 0], fg_buf.at[layer, 1], FG + 2 * layer, FG + 2 * layer + 1, ring_dev(z, 7)
-        )
-        send_to(
-            fg_send.at[layer, 1], fg_buf.at[layer, 0], FG + 2 * layer + 1, FG + 2 * layer, ring_dev(z, 1)
-        )
+        ghosts = dot(rounded, sel[...])
+        for side in range(2):
+            pack_side(fg_send.at[layer, side], ghosts[:, SIDE * side : SIDE * (side + 1)])
+        send_sides(fg_send.at[layer], fg_buf.at[layer], FG + 2 * layer)
 
     def receive_features(layer):
         for side in range(2):
             arrive(fg_buf.at[layer, side], FG + 2 * layer + side)
-            ext_rows[:, ATOMS + SIDE * side : ATOMS + SIDE * (side + 1)] = fg_buf[layer, side]
+            unpack_side(ext_rows, fg_buf.at[layer, side], ATOMS + SIDE * side)
 
     arrive(emb_buf, EMB)
     rounded = emb_buf[...]
@@ -411,8 +428,7 @@
 
         lax.fori_loop(0, NEIGH, body, 0, unroll=True)
 
-    receive_features(0)
-    gather_part(0, 0, EXT, True)
+    gather_part(0, 0, ATOMS, True)
 
     for dz in range(1, 4):
         arrive(ma_buf.at[(z + dz) % 4], MA + (z + dz) % 4)
@@ -427,8 +443,9 @@
             got = lane_pick(blocks, send_index[:, 128 * n : 128 * n + 128])
             gh_send[n // 2, c : c + 1, 128 * (n % 2) : 128 * (n % 2) + 128] = got[0:1]
     gh_send[:, 3:4, :] = jnp.zeros((2, 1, SIDE), F32)
-    send_to(gh_send.at[0], gh_buf.at[1], GH, GH + 1, ring_dev(z, 7))
-    send_to(gh_send.at[1], gh_buf.at[0], GH + 1, GH, ring_dev(z, 1))
+    send_sides(gh_send, gh_buf, GH)
+    receive_features(0)
+    gather_part(0, ATOMS, EXT, False)
     turns = centre * 0.25
     high = turns.astype(BF16).astype(F32)
     rest = turns - high
@@ -469,12 +486,11 @@
             cos_buf[pl.ds(at, 128), :] = (1.0 - 2.0 * s * s).astype(BF16)
             return carry
 
-        lax.fori_loop(0, KPART // 128, body, 0)
+        lax.fori_loop(0, KPART // 128, body, 0, unroll=True)
         weights = stacked_parts(jnp.broadcast_to(charges, (8, ATOMS)))
         for number, ref in enumerate((cos_buf, sin_buf)):
             sums = dot_t(weights, ref[...])
             sa_buf[core, number : number + 1, :] = sums[0:1] + sums[8:9]
-        send_to(sa_buf.at[core], sa_buf.at[core], SA, SA, dev(z, x, y, low, 1 - core))
 
     def ewald_ring():
         arrive(sa_buf.at[1 - core], SA)
@@ -487,6 +503,7 @@
     for side in range(2):
         arrive(gh_buf.at[side], GH + side)
         ghosts_at.append(gh_buf[side])
+    send_to(sa_buf.at[core], sa_buf.at[core], SA, SA, dev(z, x, y, low, 1 - core))
     index8 = pack_buf[0:8, :].astype(jnp.int32)
     distance = None
     for c in range(3):
@@ -620,19 +637,23 @@
         return carry
 
     lax.fori_loop(0, NEIGH, row_cotan, 0, unroll=True)
-    for side in range(2):
-        first = ATOMS + SIDE * side
-        dg_send[side] = dot_t(d_picked[...], onehot[first : first + SIDE, :]).astype(BF16)
-        send_to(dg_send.at[side], dg_buf.at[1 - side], DG + side, DG + 1 - side, ring_dev(z, 7 if side == 0 else 1))
+    for near in range(2):
+        side = core if near == 0 else 1 - core
+        first = pl.multiple_of(ATOMS + SIDE * side, SIDE)
+        pack_side(dg_send.at[side], dot_t(d_picked[...], onehot[pl.ds(first, SIDE), :]))
+        send_to(dg_send.at[side], dg_buf.at[1 - side], DG + side, DG + 1 - side, ring_dev(z, 7 - 6 * side))
     for half in range(2):
         drows[:, SIDE * half : SIDE * half + SIDE] = dot_t(
             d_picked[...], onehot[SIDE * half : SIDE * half + SIDE, :]
         )
     distance_cotan(1)
     ewald_group_sum()
+    for near in (1, 0):
+        side = core if near == 0 else 1 - core
+        arrive(dg_buf.at[side], DG + side)
     for side in range(2):
-        arrive(dg_buf.at[side], DG + side)
-    returned = dot_t(dg_buf[0], sel[:, :SIDE]) + dot_t(dg_buf[1], sel[:, SIDE:])
+        unpack_side(dg_rows, dg_buf.at[side], SIDE * side)
+    returned = dot_t(dg_rows[...], sel[...])
     owned = (drows[...] + returned).astype(BF16).astype(F32)
     message_cotan(0, (cotan.astype(F32) + owned).astype(BF16))
     distance_cotan(0)
@@ -729,10 +750,11 @@
         ((4, 4, ATOMS), F32),
         ((2, 4, SIDE), F32),
         ((2, 4, SIDE), F32),
-        ((2, 2, FEAT, SIDE), BF16),
-        ((2, 2, FEAT, SIDE), BF16),
-        ((2, FEAT, SIDE), BF16),
-        ((2, FEAT, SIDE), BF16),
+        ((2, 2, PACKED, 128), BF16),
+        ((2, 2, PACKED, 128), BF16),
+        ((2, PACKED, 128), BF16),
+        ((2, PACKED, 128), BF16),
+        ((FEAT, 2 * SIDE), BF16),
         ((2, 2, KPART), F32),
         ((4, 2, KPART), F32),
         ((8, 4, ATOMS), F32),

time: 50.9 us -> 47.5 us (0.933)
  Pallas kernels: 48.7 us -> 45.4 us
    pallas_call x1, Pallas kernels: 48.7 us -> 45.4 us  [local(): pl.pallas_call(step_kernel, out_shape=jax.ShapeDtypeStruct((9, 1, ATOMS),...]
where the time goes in v3:
time: 47.5 us; the launch traced here: 47.4 us
  Pallas kernels  45.4 us (96%)
  local copies, waits for them, and re-layouts  1.33 us (3%)
  between operations  0.65 us (1%)
    pallas_call x1, Pallas kernels, local(): pl.pallas_call(step_kernel, out_shape=jax.ShapeDtypeStruct((9, 1, ATOMS),...  45.4 us
    slice x1, local copies, waits for them, and re-layouts, local(): return (out[0:3], out[3:6], out[6:9])  1.33 us

profile of v3, /device:TPU:1, one launch (start us, length us, event | category | flops | bytes accessed | tf_op | source)
XLA Modules:
  0.0 47.4 jit_solution(10441420362413699462)
XLA Ops:
  0.6 45.4 %shard_map.166 = f32[9,1,512]{2,1,0:T(1,128)} custom-call(f32[96]{0:T(128)} %constant.2.clone.coef_in, f32[3,1,512]{2,1,0:T(1,128)} %pos_in.1, f32[3,1,512]{2,1,0:T(1,128)} %mom_in.1, f32[3,1,512]{2,1,0:T(1,128)} %force_in.1, f32[1,512]{1,0:T(1,128)} %bitcast.6, f32[1,512]{1,0:T(1,128)} %bitcast.7, bf16[240,512]{1,0:T(8,128)(2,1)} %bitcast.5, ...), custom_call_target="tpu_custom_call" | custom-call | flops 16000000000 | bytes 2000000 | tf_op jit(solution)/shard_map/pallas_call | solution.py:796
  46.0 1.3 %fusion = (f32[3,1,512]{2,1,0:T(1,128)}, f32[3,1,512]{2,1,0:T(1,128)}, f32[3,1,512]{2,1,0:T(1,128)}) fusion(f32[9,1,512]{2,1,0:T(1,128)} %shard_map.166), kind=kLoop, calls=%fused_computation | loop fusion | bytes 36864 | tf_op jit(solution)/shard_map/slice | solution.py:829

commit v4 on v3

--- a/solution.py
+++ b/solution.py
@@ -28,7 +28,7 @@
 PACKED = FEAT + 128
 
 S1, EMB, PACK, MA, MB, GH, FG, DG, SA, SB, E1, E2, XP, FO, GG, N_SEMS = np.cumsum(
-    [0, 8, 1, 1, 4, 4, 2, 4, 2, 1, 4, 8, 4, 1, 1, 2]
+    [0, 8, 1, 1, 4, 4, 2, 4, 2, 1, 4, 4, 8, 1, 1, 2]
 ).tolist()
 
 
@@ -133,6 +133,7 @@
     sa_buf,
     sb_buf,
     e1_buf,
+    e2_send,
     e2_buf,
     xp_send,
     xp_buf,
@@ -229,7 +230,8 @@
         )
     ):
         loads[number] = pltpu.make_async_copy(src, dst, load_sem.at[number])
-        loads[number].start()
+        if number < 7:
+            loads[number].start()
 
     same = low == core
     conditional = []
@@ -267,6 +269,9 @@
     greet(ring_dev(z, 7 - 6 * core))
     greet(dev(z, x, y, core, 1 - low))
     greet(ring_dev(z, 1 + 6 * core))
+
+    for number in range(7, 14):
+        loads[number].start()
 
     for number in range(7):
         loads[number].wait()
@@ -491,6 +496,7 @@
         for number, ref in enumerate((cos_buf, sin_buf)):
             sums = dot_t(weights, ref[...])
             sa_buf[core, number : number + 1, :] = sums[0:1] + sums[8:9]
+        send_to(sa_buf.at[core], sa_buf.at[core], SA, SA, dev(z, x, y, low, 1 - core))
 
     def ewald_ring():
         arrive(sa_buf.at[1 - core], SA)
@@ -498,12 +504,10 @@
         for dy in range(1, 4):
             send_to(sb_buf.at[y], sb_buf.at[y], SB + dy, SB + y, dev(z, x, (y + dy) % 4, low, core))
 
-    ewald_sums()
     ghosts_at = []
     for side in range(2):
         arrive(gh_buf.at[side], GH + side)
         ghosts_at.append(gh_buf[side])
-    send_to(sa_buf.at[core], sa_buf.at[core], SA, SA, dev(z, x, y, low, 1 - core))
     index8 = pack_buf[0:8, :].astype(jnp.int32)
     distance = None
     for c in range(3):
@@ -537,33 +541,26 @@
         from_cos = stacked_parts(recip * (damping * sums[1:2]))
         part = dot(from_sin, sin_buf[...]) - dot(from_cos, cos_buf[...])
         part = 2.0 * charges * (part[0:8] + part[8:16])
-        place = 2 * x + low
-        e1_buf[place] = part[0:4]
-        for number in range(1, 8):
-            dx, dl = number // 2, number % 2
-            send_to(
-                e1_buf.at[place],
-                e1_buf.at[place],
-                E1 + number,
-                E1 + place,
-                dev(z, (x + dx) % 4, y, (low + dl) % 2, core),
-            )
+        e1_buf[x] = part[0:4]
+        for dx in (2, 1, 3):
+            send_to(e1_buf.at[x], e1_buf.at[x], E1 + dx, E1 + x, dev(z, (x + dx) % 4, y, low, core))
 
     def ewald_group_sum():
-        for number in range(1, 8):
-            place = 2 * ((x + number // 2) % 4) + (low + number % 2) % 2
-            arrive(e1_buf.at[place], E1 + place)
-        part = e1_buf[0]
-        for k in range(1, 8):
-            part = part + e1_buf[k]
-        e2_buf[z] = part
-        for dz in range(1, 4):
-            send_to(e2_buf.at[z], e2_buf.at[z], E2 + dz, E2 + z, ring_dev((z + dz) % 4, 0))
-
-    def ewald_total():
-        for dz in range(1, 4):
-            arrive(e2_buf.at[(z + dz) % 4], E2 + (z + dz) % 4)
-        return (e2_buf[0] + e2_buf[1]) + (e2_buf[2] + e2_buf[3])
+        for dx in (1, 3, 2):
+            arrive(e1_buf.at[(x + dx) % 4], E1 + (x + dx) % 4)
+        e2_send[...] = (e1_buf[0] + e1_buf[1]) + (e1_buf[2] + e1_buf[3])
+        place = 2 * z + low
+        for dz in (2, 1, 3, 0):
+            for flip in (1, 0):
+                if dz or flip:
+                    send_to(
+                        e2_send,
+                        e2_buf.at[place],
+                        E2 + 2 * dz + flip,
+                        E2 + place,
+                        dev((z + dz) % 4, x, y, core, (low + flip) % 2),
+                    )
+        send_or_keep(e2_send, e2_buf.at[place], E2, E2 + place, swap)
 
     def finish_layer(layer):
         msg[...] = jnp.zeros((FEAT, ATOMS), F32)
@@ -584,17 +581,17 @@
         gated = (pre * lax.logistic(pre)).astype(BF16)
         hidden[...] += dot(update_t[layer], gated)
 
-    ewald_ring()
     finish_layer(0)
     rounded = hidden[...].astype(BF16)
     ext_rows[:, :ATOMS] = rounded
     send_features(1, rounded)
+    ewald_sums()
     gather_part(1, 0, ATOMS, True)
+    ewald_ring()
     for dz in range(1, 4):
         arrive(mb_buf.at[(z + dz) % 4], MB + (z + dz) % 4)
     xp_send[4:8, :] = (mb_buf[0] + mb_buf[1]) + (mb_buf[2] + mb_buf[3])
     send_or_keep(xp_send, xp_buf, XP, XP, swap)
-    ewald_forces()
     receive_features(1)
     gather_part(1, ATOMS, EXT, False)
     finish_layer(1)
@@ -642,12 +639,12 @@
         first = pl.multiple_of(ATOMS + SIDE * side, SIDE)
         pack_side(dg_send.at[side], dot_t(d_picked[...], onehot[pl.ds(first, SIDE), :]))
         send_to(dg_send.at[side], dg_buf.at[1 - side], DG + side, DG + 1 - side, ring_dev(z, 7 - 6 * side))
+    ewald_forces()
     for half in range(2):
         drows[:, SIDE * half : SIDE * half + SIDE] = dot_t(
             d_picked[...], onehot[SIDE * half : SIDE * half + SIDE, :]
         )
     distance_cotan(1)
-    ewald_group_sum()
     for near in (1, 0):
         side = core if near == 0 else 1 - core
         arrive(dg_buf.at[side], DG + side)
@@ -657,6 +654,7 @@
     owned = (drows[...] + returned).astype(BF16).astype(F32)
     message_cotan(0, (cotan.astype(F32) + owned).astype(BF16))
     distance_cotan(0)
+    ewald_group_sum()
 
     ddist = 2.0 * ddist_buf[...]
     edge_force = [offset_buf[c] * ddist for c in range(3)]
@@ -671,15 +669,16 @@
         rows = [edge_force[c][j : j + 1, :] for c in range(3)] + [zero_row] * 5
         parts.append(stacked_parts(jnp.concatenate(rows, 0)))
     force_rows = jnp.concatenate(parts, 1)
-    for side in range(2):
-        first = ATOMS + SIDE * side
-        both = dot_t(force_rows, onehot[first : first + SIDE, :])
+    for near in range(2):
+        side = core if near == 0 else 1 - core
+        first = pl.multiple_of(ATOMS + SIDE * side, SIDE)
+        both = dot_t(force_rows, onehot[pl.ds(first, SIDE), :])
         gg_send[side] = both[0:4] + both[8:12]
         send_to(
-            gg_send.at[side], gg_buf.at[1 - side], GG + side, GG + 1 - side, swapped_ring_dev(7 if side == 0 else 1)
+            gg_send.at[side], gg_buf.at[1 - side], GG + side, GG + 1 - side, swapped_ring_dev(7 - 6 * side)
         )
     both = dot_t(force_rows, onehot[:ATOMS, :])
-    fo_send[...] = (fo_send[...] - (both[0:4] + both[8:12])) + ewald_total()
+    fo_send[...] = fo_send[...] - (both[0:4] + both[8:12])
     send_or_keep(fo_send, fo_buf, FO, FO, swap)
 
     arrive(xp_buf, XP)
@@ -693,7 +692,12 @@
         both = both[0:4] + both[8:12]
         returned = both if side == 0 else returned + both
     arrive(fo_buf, FO)
-    result = fo_buf[...] - returned
+    for place in range(8):
+        arrive(e2_buf.at[place], E2 + place)
+    long_range = e2_buf[0]
+    for place in range(1, 8):
+        long_range = long_range + e2_buf[place]
+    result = (fo_buf[...] - returned) + long_range
     for c in range(3):
         out[c] = xp_buf[c : c + 1, :]
         out[3 + c] = xp_buf[4 + c : 5 + c, :] + (0.5 * DT) * result[c : c + 1, :]
@@ -757,8 +761,9 @@
         ((FEAT, 2 * SIDE), BF16),
         ((2, 2, KPART), F32),
         ((4, 2, KPART), F32),
+        ((4, 4, ATOMS), F32),
+        ((4, ATOMS), F32),
         ((8, 4, ATOMS), F32),
-        ((4, 4, ATOMS), F32),
         ((8, ATOMS), F32),
         ((8, ATOMS), F32),
         ((4, ATOMS), F32),

time: 47.5 us -> 46.6 us (0.981)
  Pallas kernels: 45.4 us -> 44.4 us
    pallas_call x1, Pallas kernels: 45.4 us -> 44.4 us  [local(): pl.pallas_call(step_kernel, out_shape=jax.ShapeDtypeStruct((9, 1, ATOMS),...]
where the time goes in v4:
time: 46.6 us; the launch traced here: 46.4 us
  Pallas kernels  44.4 us (95%)
  local copies, waits for them, and re-layouts  1.33 us (3%)
  between operations  0.65 us (1%)
    pallas_call x1, Pallas kernels, local(): pl.pallas_call(step_kernel, out_shape=jax.ShapeDtypeStruct((9, 1, ATOMS),...  44.4 us
    slice x1, local copies, waits for them, and re-layouts, local(): return (out[0:3], out[3:6], out[6:9])  1.33 us

profile of v4, /device:TPU:1, one launch (start us, length us, event | category | flops | bytes accessed | tf_op | source)
XLA Modules:
  0.0 46.4 jit_solution(9531677751308076096)
XLA Ops:
  0.6 44.4 %shard_map.166 = f32[9,1,512]{2,1,0:T(1,128)} custom-call(f32[96]{0:T(128)} %constant.2.clone.coef_in, f32[3,1,512]{2,1,0:T(1,128)} %pos_in.1, f32[3,1,512]{2,1,0:T(1,128)} %mom_in.1, f32[3,1,512]{2,1,0:T(1,128)} %force_in.1, f32[1,512]{1,0:T(1,128)} %bitcast.6, f32[1,512]{1,0:T(1,128)} %bitcast.7, bf16[240,512]{1,0:T(8,128)(2,1)} %bitcast.5, ...), custom_call_target="tpu_custom_call" | custom-call | flops 16000000000 | bytes 2000000 | tf_op jit(solution)/shard_map/pallas_call | solution.py:801
  45.1 1.3 %fusion = (f32[3,1,512]{2,1,0:T(1,128)}, f32[3,1,512]{2,1,0:T(1,128)}, f32[3,1,512]{2,1,0:T(1,128)}) fusion(f32[9,1,512]{2,1,0:T(1,128)} %shard_map.166), kind=kLoop, calls=%fused_computation | loop fusion | bytes 36864 | tf_op jit(solution)/shard_map/slice | solution.py:834

commit v5 on v4

--- a/solution.py
+++ b/solution.py
@@ -28,7 +28,7 @@
 PACKED = FEAT + 128
 
 S1, EMB, PACK, MA, MB, GH, FG, DG, SA, SB, E1, E2, XP, FO, GG, N_SEMS = np.cumsum(
-    [0, 8, 1, 1, 4, 4, 2, 4, 2, 1, 4, 4, 8, 1, 1, 2]
+    [0, 8, 1, 1, 8, 8, 2, 4, 2, 1, 4, 4, 8, 1, 1, 2]
 ).tolist()
 
 
@@ -256,18 +256,20 @@
 
     far = dev((z + 3 + 2 * low) % 4, x, y, 1 - low, low)
     for dz in (2, 1, 3):
-        greet(dev((z + dz) % 4, x, y, low, core))
+        greet(dev((z + dz) % 4, x, y, core, core))
     greet(ring_dev(z, 4))
-    for dx, flip in ((2, 1), (2, 0), (1, 1), (3, 1), (1, 0), (3, 0)):
-        greet(dev(z, (x + dx) % 4, y, core, (low + flip) % 2))
+
+    @pl.when(same)
+    def _():
+        for dx, flip in ((2, 1), (2, 0), (1, 1), (3, 1), (1, 0), (3, 0), (0, 1)):
+            greet(dev(z, (x + dx) % 4, y, core, (low + flip) % 2))
 
     @pl.when(jnp.logical_not(same))
     def _():
         greet(far)
-        greet(dev(z, x, y, core, low))
+        greet(dev(z, x, y, core, core))
 
     greet(ring_dev(z, 7 - 6 * core))
-    greet(dev(z, x, y, core, 1 - low))
     greet(ring_dev(z, 1 + 6 * core))
 
     for number in range(7, 14):
@@ -295,17 +297,11 @@
     pack_own[9:10, :] = charge[...]
     pack_own[10:11, :] = spread
     pack_own[11:16, :] = jnp.zeros((5, ATOMS), F32)
-    pl.semaphore_wait(barrier, 13 + 2 * jnp.where(same, 0, 1))
+    pl.semaphore_wait(barrier, jnp.where(same, 13, 8))
 
     slot = x * 2 + core
-    for dx, dl in ((2, 1), (2, 0), (1, 1), (3, 1), (1, 0), (3, 0), (0, 1)):
-        send_to(
-            v_own,
-            v_all.at[slot],
-            S1 + 2 * dx + dl,
-            S1 + slot,
-            dev(z, (x + dx) % 4, y, (low + dl) % 2, low),
-        )
+    for dx in (2, 1, 3):
+        send_to(v_own, v_all.at[slot], S1 + dx, S1 + slot, dev(z, (x + dx) % 4, y, low, low))
     send_or_keep(v_own, v_all.at[slot], S1, S1 + slot, dev(z, x, y, low, low))
     swap = dev(z, x, y, core, low)
     send_or_keep(pack_own, pack_buf, PACK, PACK, far)
@@ -332,42 +328,58 @@
     wave_t[...] = jnp.transpose(wave_buf[...]).astype(BF16)
 
     arrive(pack_buf, PACK)
-    inv_mass = 1.0 / pack_buf[8:9, :]
     charges = pack_buf[9:10, :]
     send_row = pack_buf[10:11, :]
     sel[...] = jnp.where(jnp.broadcast_to(send_row, (ATOMS, 2 * SIDE)) == atom_rows, 1.0, 0.0).astype(BF16)
     send_index = jnp.broadcast_to(send_row, (8, 2 * SIDE)).astype(jnp.int32)
 
-    for k in range(8):
-        arrive(v_all.at[k], S1 + k)
     row8 = rows_of((8, ATOMS))
-    upper = row8 < 4
-    scale = jnp.where(upper, inv_mass, -pack_buf[8:9, :])
-    beads_in = [v_all[k] for k in range(8)]
-    total = beads_in[0]
-    for k in range(1, 8):
-        total = total + beads_in[k]
-    centre_part = (total + DT * inv_mass * pltpu.roll(total, 4, 0)) * (1.0 / BEADS)
-    centre_low = pltpu.roll(centre_part, 4, 0)
-    first_row = rows_of((8, 1)) < 4
-    for dz in (2, 1, 3, 0):
-        z_to = (z + dz) % 4
-        straight = None
+    targets = [(2, 0), (2, 1), (1, 0), (3, 0), (1, 1), (3, 1), (0, 1), (0, 0)]
+
+    def sums_copy(number, src, dst, first_sem):
+        target = dev((z + number // 2) % 4, x, y, (low + number % 2) % 2, core)
+        return copy(src.at[number], dst.at[z], first_sem + number, first_sem + z, target)
+
+    @pl.when(same)
+    def _():
         for k in range(8):
-            shift = (8 * (z_to - z) + 2 * x + low - k + 64) % BEADS
-            same_kind = coef[shift] * beads_in[k]
-            other = jnp.where(first_row, coef[2 * BEADS + shift], coef[BEADS + shift]) * beads_in[k]
-            straight = same_kind if straight is None else straight + same_kind
-            crossed = other if k == 0 else crossed + other
-        moved = straight + scale * pltpu.roll(crossed, 4, 0)
-        ma = jnp.where(upper, moved, centre_low)
-        if dz:
-            ma_send[dz] = ma
-            mb_send[dz] = moved[4:8]
-            send_to(ma_send.at[dz], ma_buf.at[z], MA + dz, MA + z, ring_dev(z_to, 0))
-        else:
-            ma_buf[z] = ma
-            mb_buf[z] = moved[4:8]
+            arrive(v_all.at[k], S1 + k)
+        upper = row8 < 4
+        inv_mass = 1.0 / mass[...]
+        scale = jnp.where(upper, inv_mass, -mass[...])
+        beads_in = [v_all[k] for k in range(8)]
+        total = beads_in[0]
+        for k in range(1, 8):
+            total = total + beads_in[k]
+        centre_part = (total + DT * inv_mass * pltpu.roll(total, 4, 0)) * (1.0 / BEADS)
+        centre_low = pltpu.roll(centre_part, 4, 0)
+        first_row = rows_of((8, 1)) < 4
+        for dz, flip in targets:
+            z_to, low_to, number = (z + dz) % 4, (low + flip) % 2, 2 * dz + flip
+            straight = None
+            for k in range(8):
+                shift = (8 * (z_to - z) + 2 * x + low_to - k + 64) % BEADS
+                same_kind = coef[shift] * beads_in[k]
+                other = jnp.where(first_row, coef[2 * BEADS + shift], coef[BEADS + shift]) * beads_in[k]
+                straight = same_kind if k == 0 else straight + same_kind
+                crossed = other if k == 0 else crossed + other
+            moved = straight + scale * pltpu.roll(crossed, 4, 0)
+            ma = jnp.where(upper, moved, centre_low)
+            if number:
+                ma_send[number] = ma
+                mb_send[number] = moved[4:8]
+                sums_copy(number, ma_send, ma_buf, MA).start()
+            else:
+                ma_buf[z] = ma
+                mb_buf[z] = moved[4:8]
+
+    def arrive_sums(buf, first_sem):
+        @pl.when(jnp.logical_not(same))
+        def _():
+            arrive(buf.at[z], first_sem + z)
+
+        for dz in (1, 3, 2):
+            arrive(buf.at[(z + dz) % 4], first_sem + (z + dz) % 4)
 
     def pack_side(ref, value):
         ref[0:FEAT, :] = value[:, 0:128].astype(BF16)
@@ -403,8 +415,11 @@
     hidden[...] = rounded.astype(F32)
     ext_rows[:, :ATOMS] = rounded
     send_features(0, rounded)
-    for dz in range(1, 4):
-        send_to(mb_send.at[dz], mb_buf.at[z], MB + dz, MB + z, ring_dev((z + dz) % 4, 0))
+
+    @pl.when(same)
+    def _():
+        for dz, flip in targets[:7]:
+            sums_copy(2 * dz + flip, mb_send, mb_buf, MB).start()
 
     group_rows = [(rows_of((16, ATOMS)) + 16 * g).astype(F32) for g in range(8)]
 
@@ -435,8 +450,7 @@
 
     gather_part(0, 0, ATOMS, True)
 
-    for dz in range(1, 4):
-        arrive(ma_buf.at[(z + dz) % 4], MA + (z + dz) % 4)
+    arrive_sums(ma_buf, MA)
     moved = (ma_buf[0] + ma_buf[1]) + (ma_buf[2] + ma_buf[3])
     centre = moved[4:7]
     xp_send[...] = moved
@@ -588,8 +602,7 @@
     ewald_sums()
     gather_part(1, 0, ATOMS, True)
     ewald_ring()
-    for dz in range(1, 4):
-        arrive(mb_buf.at[(z + dz) % 4], MB + (z + dz) % 4)
+    arrive_sums(mb_buf, MB)
     xp_send[4:8, :] = (mb_buf[0] + mb_buf[1]) + (mb_buf[2] + mb_buf[3])
     send_or_keep(xp_send, xp_buf, XP, XP, swap)
     receive_features(1)
@@ -710,6 +723,12 @@
     def _():
         for sent in conditional:
             sent.wait_send()
+
+    @pl.when(same)
+    def _():
+        for dz, flip in targets[:7]:
+            sums_copy(2 * dz + flip, ma_send, ma_buf, MA).wait_send()
+            sums_copy(2 * dz + flip, mb_send, mb_buf, MB).wait_send()
 
 
 def local(
@@ -748,9 +767,9 @@
         ((FEAT, ATOMS), BF16),
         ((16, ATOMS), F32),
         ((16, ATOMS), F32),
+        ((8, 8, ATOMS), F32),
         ((4, 8, ATOMS), F32),
-        ((4, 8, ATOMS), F32),
-        ((4, 4, ATOMS), F32),
+        ((8, 4, ATOMS), F32),
         ((4, 4, ATOMS), F32),
         ((2, 4, SIDE), F32),
         ((2, 4, SIDE), F32),

time: 46.6 us -> 46.3 us (level)
  no operation moved by 1% of the time
where the time goes in v5:
time: 46.3 us; the launch traced here: 46.1 us
  Pallas kernels  44.1 us (95%)
  local copies, waits for them, and re-layouts  1.33 us (3%)
  between operations  0.65 us (1%)
    pallas_call x1, Pallas kernels, local(): pl.pallas_call(step_kernel, out_shape=jax.ShapeDtypeStruct((9, 1, ATOMS),...  44.1 us
    slice x1, local copies, waits for them, and re-layouts, local(): return (out[0:3], out[3:6], out[6:9])  1.33 us

profile of v5, /device:TPU:1, one launch (start us, length us, event | category | flops | bytes accessed | tf_op | source)
XLA Modules:
  0.0 46.1 jit_solution(12393219449586207886)
XLA Ops:
  0.6 44.1 %shard_map.166 = f32[9,1,512]{2,1,0:T(1,128)} custom-call(f32[96]{0:T(128)} %constant.2.clone.coef_in, f32[3,1,512]{2,1,0:T(1,128)} %pos_in.1, f32[3,1,512]{2,1,0:T(1,128)} %mom_in.1, f32[3,1,512]{2,1,0:T(1,128)} %force_in.1, f32[1,512]{1,0:T(1,128)} %bitcast.6, f32[1,512]{1,0:T(1,128)} %bitcast.7, bf16[240,512]{1,0:T(8,128)(2,1)} %bitcast.5, ...), custom_call_target="tpu_custom_call" | custom-call | flops 16000000000 | bytes 2000000 | tf_op jit(solution)/shard_map/pallas_call | solution.py:820
  44.8 1.3 %fusion = (f32[3,1,512]{2,1,0:T(1,128)}, f32[3,1,512]{2,1,0:T(1,128)}, f32[3,1,512]{2,1,0:T(1,128)}) fusion(f32[9,1,512]{2,1,0:T(1,128)} %shard_map.166), kind=kLoop, calls=%fused_computation | loop fusion | bytes 36864 | tf_op jit(solution)/shard_map/slice | solution.py:853

commit v6 on v5

--- a/solution.py
+++ b/solution.py
@@ -230,7 +230,7 @@
         )
     ):
         loads[number] = pltpu.make_async_copy(src, dst, load_sem.at[number])
-        if number < 7:
+        if number < 3:
             loads[number].start()
 
     same = low == core
@@ -272,15 +272,25 @@
     greet(ring_dev(z, 7 - 6 * core))
     greet(ring_dev(z, 1 + 6 * core))
 
-    for number in range(7, 14):
+    for number in range(3, 7):
         loads[number].start()
 
-    for number in range(7):
+    for number in range(3):
         loads[number].wait()
     v_own[...] = jnp.zeros((8, ATOMS), F32)
     for c in range(3):
         v_own[c : c + 1, :] = pos[c]
         v_own[4 + c : 5 + c, :] = mom[c] + (0.5 * DT) * force[c]
+    pl.semaphore_wait(barrier, jnp.where(same, 13, 8))
+
+    slot = x * 2 + core
+    for dx in (2, 1, 3):
+        send_to(v_own, v_all.at[slot], S1 + dx, S1 + slot, dev(z, (x + dx) % 4, y, low, low))
+    send_or_keep(v_own, v_all.at[slot], S1, S1 + slot, dev(z, x, y, low, low))
+    for number in range(7, 14):
+        loads[number].start()
+    for number in range(3, 7):
+        loads[number].wait()
     lane = lanes_of((1, 2 * SIDE))
     rows384 = jnp.concatenate(
         [send[0:1, :], send[1:2, :], send[2:3, :], jnp.zeros((1, 128), jnp.int32)], 1
@@ -297,12 +307,6 @@
     pack_own[9:10, :] = charge[...]
     pack_own[10:11, :] = spread
     pack_own[11:16, :] = jnp.zeros((5, ATOMS), F32)
-    pl.semaphore_wait(barrier, jnp.where(same, 13, 8))
-
-    slot = x * 2 + core
-    for dx in (2, 1, 3):
-        send_to(v_own, v_all.at[slot], S1 + dx, S1 + slot, dev(z, (x + dx) % 4, y, low, low))
-    send_or_keep(v_own, v_all.at[slot], S1, S1 + slot, dev(z, x, y, low, low))
     swap = dev(z, x, y, core, low)
     send_or_keep(pack_own, pack_buf, PACK, PACK, far)
     send_or_keep(emb, emb_buf, EMB, EMB, far)

time: 46.3 us -> 46.3 us (level)
  no operation moved by 1% of the time
where the time goes in v6:
time: 46.3 us; the launch traced here: 46.1 us
  Pallas kernels  44.2 us (95%)
  local copies, waits for them, and re-layouts  1.33 us (3%)
  between operations  0.65 us (1%)
    pallas_call x1, Pallas kernels, local(): pl.pallas_call(step_kernel, out_shape=jax.ShapeDtypeStruct((9, 1, ATOMS),...  44.2 us
    slice x1, local copies, waits for them, and re-layouts, local(): return (out[0:3], out[3:6], out[6:9])  1.33 us

profile of v6, /device:TPU:1, one launch (start us, length us, event | category | flops | bytes accessed | tf_op | source)
XLA Modules:
  0.0 46.1 jit_solution(9252726743191757011)
XLA Ops:
  0.6 44.2 %shard_map.166 = f32[9,1,512]{2,1,0:T(1,128)} custom-call(f32[96]{0:T(128)} %constant.2.clone.coef_in, f32[3,1,512]{2,1,0:T(1,128)} %pos_in.1, f32[3,1,512]{2,1,0:T(1,128)} %mom_in.1, f32[3,1,512]{2,1,0:T(1,128)} %force_in.1, f32[1,512]{1,0:T(1,128)} %bitcast.6, f32[1,512]{1,0:T(1,128)} %bitcast.7, bf16[240,512]{1,0:T(8,128)(2,1)} %bitcast.5, ...), custom_call_target="tpu_custom_call" | custom-call | flops 16000000000 | bytes 2000000 | tf_op jit(solution)/shard_map/pallas_call | solution.py:824
  44.8 1.3 %fusion = (f32[3,1,512]{2,1,0:T(1,128)}, f32[3,1,512]{2,1,0:T(1,128)}, f32[3,1,512]{2,1,0:T(1,128)}) fusion(f32[9,1,512]{2,1,0:T(1,128)} %shard_map.166), kind=kLoop, calls=%fused_computation | loop fusion | bytes 36864 | tf_op jit(solution)/shard_map/slice | solution.py:857

commit v7 on v5

--- a/solution.py
+++ b/solution.py
@@ -333,6 +333,18 @@
     sel[...] = jnp.where(jnp.broadcast_to(send_row, (ATOMS, 2 * SIDE)) == atom_rows, 1.0, 0.0).astype(BF16)
     send_index = jnp.broadcast_to(send_row, (8, 2 * SIDE)).astype(jnp.int32)
 
+    def finish_sends(always, if_apart):
+        for sent in always:
+            sent.wait_send()
+        always.clear()
+
+        @pl.when(jnp.logical_not(same))
+        def _():
+            for sent in if_apart:
+                sent.wait_send()
+
+        if_apart.clear()
+
     row8 = rows_of((8, ATOMS))
     targets = [(2, 0), (2, 1), (1, 0), (3, 0), (1, 1), (3, 1), (0, 1), (0, 0)]
 
@@ -667,6 +679,9 @@
     owned = (drows[...] + returned).astype(BF16).astype(F32)
     message_cotan(0, (cotan.astype(F32) + owned).astype(BF16))
     distance_cotan(0)
+    early, early_apart = list(started), list(conditional)
+    started.clear()
+    conditional.clear()
     ewald_group_sum()
 
     ddist = 2.0 * ddist_buf[...]
@@ -693,6 +708,14 @@
     both = dot_t(force_rows, onehot[:ATOMS, :])
     fo_send[...] = fo_send[...] - (both[0:4] + both[8:12])
     send_or_keep(fo_send, fo_buf, FO, FO, swap)
+
+    finish_sends(early, early_apart)
+
+    @pl.when(same)
+    def _():
+        for dz, flip in targets[:7]:
+            sums_copy(2 * dz + flip, ma_send, ma_buf, MA).wait_send()
+            sums_copy(2 * dz + flip, mb_send, mb_buf, MB).wait_send()
 
     arrive(xp_buf, XP)
     for side in range(2):
@@ -716,19 +739,7 @@
         out[3 + c] = xp_buf[4 + c : 5 + c, :] + (0.5 * DT) * result[c : c + 1, :]
         out[6 + c] = result[c : c + 1, :]
 
-    for sent in started:
-        sent.wait_send()
-
-    @pl.when(jnp.logical_not(same))
-    def _():
-        for sent in conditional:
-            sent.wait_send()
-
-    @pl.when(same)
-    def _():
-        for dz, flip in targets[:7]:
-            sums_copy(2 * dz + flip, ma_send, ma_buf, MA).wait_send()
-            sums_copy(2 * dz + flip, mb_send, mb_buf, MB).wait_send()
+    finish_sends(started, conditional)
 
 
 def local(

time: 46.3 us -> 46.2 us (level)
  no operation moved by 1% of the time
where the time goes in v7:
time: 46.2 us; the launch traced here: 46.1 us
  Pallas kernels  44.1 us (95%)
  local copies, waits for them, and re-layouts  1.33 us (3%)
  between operations  0.65 us (1%)
    pallas_call x1, Pallas kernels, local(): pl.pallas_call(step_kernel, out_shape=jax.ShapeDtypeStruct((9, 1, ATOMS),...  44.1 us
    slice x1, local copies, waits for them, and re-layouts, local(): return (out[0:3], out[3:6], out[6:9])  1.33 us

profile of v7, /device:TPU:1, one launch (start us, length us, event | category | flops | bytes accessed | tf_op | source)
XLA Modules:
  0.0 46.1 jit_solution(12548127572858700492)
XLA Ops:
  0.6 44.1 %shard_map.166 = f32[9,1,512]{2,1,0:T(1,128)} custom-call(f32[96]{0:T(128)} %constant.2.clone.coef_in, f32[3,1,512]{2,1,0:T(1,128)} %pos_in.1, f32[3,1,512]{2,1,0:T(1,128)} %mom_in.1, f32[3,1,512]{2,1,0:T(1,128)} %force_in.1, f32[1,512]{1,0:T(1,128)} %bitcast.6, f32[1,512]{1,0:T(1,128)} %bitcast.7, bf16[240,512]{1,0:T(8,128)(2,1)} %bitcast.5, ...), custom_call_target="tpu_custom_call" | custom-call | flops 16000000000 | bytes 2000000 | tf_op jit(solution)/shard_map/pallas_call | solution.py:831
  44.7 1.3 %fusion = (f32[3,1,512]{2,1,0:T(1,128)}, f32[3,1,512]{2,1,0:T(1,128)}, f32[3,1,512]{2,1,0:T(1,128)}) fusion(f32[9,1,512]{2,1,0:T(1,128)} %shard_map.166), kind=kLoop, calls=%fused_computation | loop fusion | bytes 36864 | tf_op jit(solution)/shard_map/slice | solution.py:864

commit v8 on v5

--- a/solution.py
+++ b/solution.py
@@ -600,13 +600,37 @@
     ext_rows[:, :ATOMS] = rounded
     send_features(1, rounded)
     ewald_sums()
-    gather_part(1, 0, ATOMS, True)
+
+    def receive_side(side):
+        arrive(fg_buf.at[1, side], FG + 2 + side)
+        packed = fg_buf.at[1, side]
+        first = pl.multiple_of(ATOMS + SIDE * side, SIDE)
+        later = pl.multiple_of(first + 128, 128)
+        ext_rows[:, pl.ds(first, 128)] = packed[0:FEAT, :]
+        rest = packed[FEAT:PACKED, :].astype(F32)
+        ext_rows[0:128, pl.ds(later, 128)] = rest.astype(BF16)
+        ext_rows[128:FEAT, pl.ds(later, 128)] = pltpu.roll(rest, 64, 1)[0 : FEAT - 128].astype(BF16)
+        return pl.ds(first, SIDE)
+
+    def gather_side(rows, with_own):
+        def body(j, carry):
+            columns = pl.ds(pl.multiple_of(j * ATOMS, ATOMS), ATOMS)
+            part = dot(ext_rows[:, rows], onehot[rows, columns])
+            if with_own:
+                part = part + dot(ext_rows[:, :ATOMS], onehot[:ATOMS, columns])
+            else:
+                part = part + picked[1, j].astype(F32)
+            picked[1, j] = part.astype(BF16)
+            return carry
+
+        lax.fori_loop(0, NEIGH, body, 0, unroll=True)
+
+    gather_side(receive_side(1 - core), True)
     ewald_ring()
     arrive_sums(mb_buf, MB)
     xp_send[4:8, :] = (mb_buf[0] + mb_buf[1]) + (mb_buf[2] + mb_buf[3])
     send_or_keep(xp_send, xp_buf, XP, XP, swap)
-    receive_features(1)
-    gather_part(1, ATOMS, EXT, False)
+    gather_side(receive_side(core), False)
     finish_layer(1)
 
     def silu_slope(pre):

time: 46.3 us -> 45.9 us (level)
  no operation moved by 1% of the time
where the time goes in v8:
time: 45.9 us; the launch traced here: 45.7 us
  Pallas kernels  43.8 us (95%)
  local copies, waits for them, and re-layouts  1.33 us (3%)
  between operations  0.65 us (1%)
    pallas_call x1, Pallas kernels, local(): pl.pallas_call(step_kernel, out_shape=jax.ShapeDtypeStruct((9, 1, ATOMS),...  43.8 us
    slice x1, local copies, waits for them, and re-layouts, local(): return (out[0:3], out[3:6], out[6:9])  1.33 us

profile of v8, /device:TPU:1, one launch (start us, length us, event | category | flops | bytes accessed | tf_op | source)
XLA Modules:
  0.0 45.7 jit_solution(9372593525626056181)
XLA Ops:
  0.6 43.8 %shard_map.166 = f32[9,1,512]{2,1,0:T(1,128)} custom-call(f32[96]{0:T(128)} %constant.2.clone.coef_in, f32[3,1,512]{2,1,0:T(1,128)} %pos_in.1, f32[3,1,512]{2,1,0:T(1,128)} %mom_in.1, f32[3,1,512]{2,1,0:T(1,128)} %force_in.1, f32[1,512]{1,0:T(1,128)} %bitcast.6, f32[1,512]{1,0:T(1,128)} %bitcast.7, bf16[240,512]{1,0:T(8,128)(2,1)} %bitcast.5, ...), custom_call_target="tpu_custom_call" | custom-call | flops 16000000000 | bytes 2000000 | tf_op jit(solution)/shard_map/pallas_call | solution.py:844
  44.4 1.3 %fusion = (f32[3,1,512]{2,1,0:T(1,128)}, f32[3,1,512]{2,1,0:T(1,128)}, f32[3,1,512]{2,1,0:T(1,128)}) fusion(f32[9,1,512]{2,1,0:T(1,128)} %shard_map.166), kind=kLoop, calls=%fused_computation | loop fusion | bytes 36864 | tf_op jit(solution)/shard_map/slice | solution.py:877
